TPU v7x, 32 devices: a whole 2x2x4 slice. The times are simulated.
32 devices in a mesh: chain: 4 (over y, core), sector: 8 (over z, x).
Axes of the slice: x: 2, y: 2, z: 4, core: 2. Of those that a mesh axis runs over, the one named last changes fastest.
Arguments:
- site_tensors: bfloat16 [8, 8, 128, 4, 128], P('chain', 'sector'), may hold values from -0.5 to 0.5
- mpo: bfloat16 [8, 42, 42, 4, 4], P('chain'), may hold values from -0.75 to 0.75
- left_in: bfloat16 [4, 8, 42, 128, 128], P('chain', 'sector'), may hold values from -6 to 6
- right_in: bfloat16 [4, 8, 42, 128, 128], P('chain', 'sector'), may hold values from -6 to 6
- tile_rows: int32 [9, 8], replicated, may hold values from 32 to 128
Outputs:
- left_envs: bfloat16 [8, 8, 42, 128, 128], P('chain', 'sector')
- right_envs: bfloat16 [8, 8, 42, 128, 128], P('chain', 'sector')
- left_edge: bfloat16 [4, 8, 42, 128, 128], P('chain', 'sector')
All inputs are finite; a program needn't handle non-finite values.
Results may differ from a plain program's by a relative error of at most 0.009.
Values may be sent and summed in bfloat16 or wider, within the bound.
No kernel may reach another device: no remote copies, remote signals or barrier semaphores. Data moves between devices by JAX's collectives and lax.ppermute only.
A program may use at most 128 MiB of HBM per device.

v0:
```python
import functools

import jax
import jax.numpy as jnp
from jax import lax
from jax.experimental import pallas as pl
from jax.experimental.pallas import tpu as pltpu
from jax.sharding import PartitionSpec as P

f32 = jnp.float32
bf16 = jnp.bfloat16
AXES = ("chain", "sector")
SUBLANES = 8
GROUP = SUBLANES // 2
STEP_ROWS = 2 * SUBLANES
ANY = pl.BlockSpec(memory_space=pl.ANY)
SMEM = pl.BlockSpec(memory_space=pltpu.SMEM)
VMEM = pl.BlockSpec(memory_space=pltpu.VMEM)
LIMIT = 18 * 2**20


class Routes:
    def __init__(self, chains, sectors):
        def at(pair, core, z, x):
            return (2 * pair + core) * sectors + 2 * z + x

        pairs, zs = range(chains // 2), range(sectors // 2)
        every = [(y, z, e) for y in pairs for z in zs for e in (0, 1)]
        below = [(y, z, e) for y, z, e in every if z + 1 in zs]
        self.left_cross = [(at(y, e, z, 1 - e), at(y, e, z, e)) for y, z, e in every]
        self.right_cross = [(at(y, e, z, 1 - e), at(y, 1 - e, z, e)) for y, z, e in every]
        self.to_right_core = [(at(y, e, z, e), at(y, 1 - e, z, e)) for y, z, e in every]
        self.left_up = [(at(y, e, z, e), at(y, e, z + 1, e)) for y, z, e in below]
        self.right_down = [(at(y, 1 - e, z + 1, e), at(y, 1 - e, z, e)) for y, z, e in below]
        self.right_native_down = [(at(y, e, z + 1, e), at(y, 1 - e, z, e)) for y, z, e in below]
        self.left_back = [(b, a) for a, b in self.left_cross]
        self.right_back = [(b, a) for a, b in self.right_cross]
        self.from_right_core = [(b, a) for a, b in self.to_right_core]
        shifts = [(c, q) for c in range(chains - 1) for q in range(sectors)]
        self.edge_same = [(c * sectors + q, (c + 1) * sectors + q) for c, q in shifts if c % 2 == q % 2]
        self.edge_other = [(c * sectors + q, (c + 1) * sectors + q) for c, q in shifts if c % 2 != q % 2]


def move(block, route):
    return lax.ppermute(block, AXES, route)


def in_hbm(x):
    return pltpu.with_memory_space_constraint(x, pltpu.HBM)


def in_vmem(x):
    return pltpu.with_memory_space_constraint(x, pltpu.VMEM)


def spread_body(width, steps, info, own, received, *outs):
    def spread(k, states, flip):
        n = len(states) * width * GROUP
        cols = 4 * width
        row = lax.broadcasted_iota(jnp.int32, (n, cols), 0) // GROUP
        col = lax.broadcasted_iota(jnp.int32, (n, cols), 1)
        pick = jnp.where(row + states[0] * width == col, 1.0, 0.0)
        if not flip:
            mid = jnp.dot(pick.astype(bf16), k, preferred_element_type=f32).astype(bf16)
            out = lax.dot_general(
                mid, pick.astype(bf16), (((1,), (1,)), ((), ())), preferred_element_type=f32
            )
        else:
            out = jnp.zeros((n, n), f32)
            group = lax.broadcasted_iota(jnp.int32, (n, width), 0) // GROUP
            inner = lax.broadcasted_iota(jnp.int32, (n, width), 1)
            tall = [jnp.where(group - i * width == inner, 1.0, 0.0).astype(bf16) for i in range(len(states))]
            for i, a in enumerate(states):
                for j, b in enumerate(states):
                    block = k[a * width : (a + 1) * width, b * width : (b + 1) * width]
                    mid = lax.dot_general(
                        tall[i], block, (((1,), (1,)), ((), ())), preferred_element_type=f32
                    ).astype(bf16)
                    out += lax.dot_general(
                        mid, tall[j], (((1,), (1,)), ((), ())), preferred_element_type=f32
                    )
        i = lax.broadcasted_iota(jnp.int32, out.shape, 0) % GROUP
        j = lax.broadcasted_iota(jnp.int32, out.shape, 1) % GROUP
        return jnp.where(i == j, out, 0.0).astype(bf16)

    def fill(source, flip):
        for step in range(steps):
            k = source[steps - 1 - step if flip else step]
            for i, states in enumerate(((0,), (1, 2), (3,))):
                outs[3 * step + i][...] = spread(k, states, flip)

    @pl.when(info[3] == 1)
    def _():
        fill(own, False)

    @pl.when(info[3] != 1)
    def _():
        fill(received, True)


def spread(info, own, received):
    steps, width = own.shape[0], own.shape[1] // 4
    n = width * GROUP
    shapes = [(n, n), (2 * n, 2 * n), (n, n)] * steps
    return pl.pallas_call(
        functools.partial(spread_body, width, steps),
        in_specs=[SMEM, VMEM, VMEM],
        out_specs=[VMEM] * len(shapes),
        out_shape=[pltpu.HBM(s, bf16) for s in shapes],
        compiler_params=pltpu.CompilerParams(vmem_limit_bytes=LIMIT),
    )(info, own, received)


def terms_body(left, last, final, onto, width, tile, step, steps, info, table, pair, pieces, a_near, a_cross, small, large, *rest):
    joined = not pieces
    if last:
        acc, *rest = rest
        if left:
            rest = rest[1:] if onto else rest
            envs, *rest = rest
            *rest, envs_sem = rest
        out_pair = out_near = None
        if not final:
            out_pair, *rest = rest
        if final or not left:
            out_near, *rest = rest
        out_cross, info_out, *rest = rest
    else:
        acc, info_out, *rest = rest
    bd, bm, cp, cq, one0, two0, one1, two1, z, vacc, an, ac, ks, kd, sem, weight_sem, *rest = rest
    first, zpos, x, same = info[0], info[1], info[2], info[3]
    for i in range(info.shape[0]):
        info_out[i] = info[i]
    active = same if left else 1 - same
    u_near = (x == 0) if left else (x == 1)
    cuts = [0, width // 6 * 2, width // 6 * 4, width]
    site = step if left else steps - 1 - step

    def carry(which, k):
        c = pl.ds(cuts[k], cuts[k + 1] - cuts[k])
        ends = (acc.at[which, c], vacc.at[which, c])
        return pltpu.make_async_copy(*(ends if last else ends[::-1]), sem.at[which, k])

    def save(k):
        c = pl.ds(cuts[k], cuts[k + 1] - cuts[k])
        return pltpu.make_async_copy((out_pair if out_near is None else out_near).at[c], envs.at[step, 0, c], envs_sem.at[k])

    carries = [carry(which, k) for k in range(3) for which in range(2)]
    saves = [save(k) for k in range(3)] if last and left else []
    factors = [
        pltpu.make_async_copy(src.at[pl.ds(src.shape[0] - 4 * (steps - site), 4)], dst, weight_sem.at[i])
        for i, (src, dst) in enumerate(((a_near, an), (a_cross, ac)))
    ]
    weights = [
        pltpu.make_async_copy(src, dst, weight_sem.at[2 + i]) for i, (src, dst) in enumerate(((small, ks), (large, kd)))
    ]
    fetches = []
    share = width // max(len(pieces), 1)
    if rest:
        near, cross, fetch_sem = rest
        for k in range(3):
            c = pl.ds(cuts[k], cuts[k + 1] - cuts[k])
            fetches.append(pltpu.make_async_copy(pair.at[c], near.at[c], fetch_sem.at[0, k]))
            if joined or len(pieces) == 1:
                src = pair.at[pl.ds(width + cuts[k], cuts[k + 1] - cuts[k])] if joined else pieces[0].at[c]
                fetches.append(pltpu.make_async_copy(src, cross.at[c], fetch_sem.at[1, k]))
        if len(pieces) > 1:
            for k, src in enumerate(pieces):
                dst = cross.at[pl.ds(k * share, share)]
                fetches.append(pltpu.make_async_copy(src, dst, fetch_sem.at[1, k]))
        crosses = [cross]
    elif joined:
        near, crosses = pair.at[pl.ds(0, width)], [pair.at[pl.ds(width, width)]]
    else:
        near, crosses = pair, [piece.at[pl.ds(0, share)] for piece in pieces]

    @pl.when(active == 1)
    def _():
        for c in factors + fetches + weights + (carries if last else []):
            c.start()
        count = table.shape[1]
        source_bond = first + (site if left else site + 1)
        target_bond = first + (site + 1 if left else site)
        sign = 1 if left else -1
        u = 2 * zpos if left else 2 * zpos + 1
        v = u + sign
        far_u, far_v = u - 2 * sign, v - 2 * sign

        def rows_of(bond, index):
            safe = jnp.clip(index, 0, count - 1)
            return jnp.where((index >= 0) & (index < count), table[bond, safe], 0)

        sub = lax.broadcasted_iota(jnp.int32, (tile, tile), 0)
        lane = lax.broadcasted_iota(jnp.int32, (tile, tile), 1)

        def factor(of_u, state, source, target):
            a = jnp.where(u_near if of_u else jnp.logical_not(u_near), an[state].astype(f32), ac[state].astype(f32))
            a = a if left else a.T
            keep = (sub < rows_of(source_bond, source)) & (lane < rows_of(target_bond, target))
            return jnp.where(keep, a, 0.0)

        for c in factors:
            c.wait()
        if last:
            dual = [factor(False, 3, far_v, v)] + [factor(not left, t, far_v, u) for t in (1, 2)]
            mono = factor(True, 3, far_u, u)
        else:
            dual = [factor(True, 0, u, u)] + [factor(left, t, u, v) for t in (1, 2)]
            mono = factor(False, 0, v, v)
        for i, m in enumerate(dual):
            bd[:, i * tile : (i + 1) * tile] = m.astype(bf16)
        bm[...] = mono.astype(bf16)
        cp[...] = dual[0].T.astype(bf16)
        for i, m in enumerate((dual[1], dual[2], mono)):
            cq[:, i * tile : (i + 1) * tile] = m.T.astype(bf16)

        dual_near = jnp.logical_not(u_near) if last else u_near

        for f in fetches:
            f.wait()
        n = width * GROUP

        def exchange(a, b):
            upper = lax.broadcasted_iota(jnp.int32, a.shape, 1) < GROUP
            return (
                jnp.where(upper, a, pltpu.roll(b, GROUP, 1)),
                jnp.where(upper, pltpu.roll(a, GROUP, 1), b),
            )

        def split(part):
            pairs = part.reshape(width // 2, 2, SUBLANES, tile)
            return jnp.concatenate([h.reshape(n, tile) for h in exchange(pairs[:, 0], pairs[:, 1])], axis=1)

        def joined_rows(part):
            part = part.reshape(width // 2, SUBLANES, 2 * tile)
            a, b = exchange(part[..., :tile], part[..., tile:])
            return jnp.stack([a, b], axis=1).reshape(width, SUBLANES, tile)

        def products(i, slots):
            one, two = slots
            r = pl.ds(pl.multiple_of(i * STEP_ROWS, STEP_ROWS), STEP_ROWS)
            e_n = near[:, r, :]
            e_c = jnp.concatenate([c[:, r, :] for c in crosses], axis=0)
            e_d = jnp.where(dual_near, e_n, e_c).reshape(width * STEP_ROWS, tile)
            e_m = jnp.where(dual_near, e_c, e_n).reshape(width * STEP_ROWS, tile)
            yd = jnp.dot(e_d, bd[...], preferred_element_type=f32).reshape(width, STEP_ROWS, 3 * tile)
            ym = jnp.dot(e_m, bm[...], preferred_element_type=f32).reshape(width, STEP_ROWS, tile)
            for h in range(2):
                c = slice(h * SUBLANES, (h + 1) * SUBLANES)
                one[2 * h] = split(yd[:, c, :tile]).astype(bf16)
                one[2 * h + 1] = split(ym[:, c, :]).astype(bf16)
                two[h] = jnp.concatenate(
                    [split(yd[:, c, t * tile : (t + 1) * tile]) for t in (1, 2)], axis=0
                ).astype(bf16)

        def mix(i, slots):
            one, two = slots
            r = pl.ds(pl.multiple_of(i * STEP_ROWS, STEP_ROWS), STEP_ROWS)

            def put(to, halves):
                z[to, :, r, :] = jnp.concatenate([joined_rows(x) for x in halves], axis=1).astype(bf16)

            for m, to in ((0, 0), (1, 3)):
                put(to, [jnp.dot(ks[...], one[2 * h + m], preferred_element_type=f32) for h in range(2)])
            mixed = [jnp.dot(kd[...], two[h], preferred_element_type=f32) for h in range(2)]
            for t in range(2):
                put(1 + t, [x[t * n : (t + 1) * n] for x in mixed])

        y0, y1 = (one0, two0), (one1, two1)
        count_rows = tile // STEP_ROWS
        products(0, y0)
        for c in weights:
            c.wait()

        def turn(j, _):
            for k in range(2 // 2):
                i = 2 * j + 2 * k
                products(i + 1, y1)
                mix(i, y0)
                products(jnp.minimum(i + 2, count_rows - 2), y0)
                mix(i + 1, y1)
            return 0

        lax.fori_loop(0, count_rows // 2, turn, 0)
        if last:
            for c in carries:
                c.wait()
        for k in range(3):
            def close(m, _, k=k):
                for i in range(7):
                    at = cuts[k] + 2 * (m * 7 + i)
                    p = jnp.dot(cp[...], jnp.concatenate([z[0, at], z[0, at + 1]], axis=1), preferred_element_type=f32)
                    zq = [z[1:4, at + n].reshape(3 * tile, tile) for n in range(2)]
                    q = jnp.dot(cq[...], jnp.concatenate(zq, axis=1), preferred_element_type=f32)
                    for n in range(2):
                        j = at + n
                        pj, qj = p[:, n * tile : (n + 1) * tile], q[:, n * tile : (n + 1) * tile]
                        if last:
                            pj, qj = pj + vacc[1, j].astype(f32), qj + vacc[0, j].astype(f32)
                            near_j = jnp.where(u_near, qj, pj).astype(bf16)
                            cross_j = jnp.where(u_near, pj, qj).astype(bf16)
                            out_cross[j] = cross_j
                            if out_near is not None:
                                out_near[j] = near_j
                            if out_pair is not None:
                                out_pair[j] = near_j
                                out_pair[width + j] = cross_j
                        else:
                            vacc[0, j] = pj.astype(bf16)
                            vacc[1, j] = qj.astype(bf16)
                return 0

            lax.fori_loop(0, (cuts[k + 1] - cuts[k]) // 14, close, 0)
            if not last:
                carries[2 * k].start()
                carries[2 * k + 1].start()
            elif left:
                saves[k].start()
        for c in saves if last else carries:
            c.wait()


def terms(left, step, steps, info, table, envs, tensors, small, large, acc=None, onto=None):
    tile = envs[0].shape[-1]
    width = small.shape[0] // GROUP
    last = acc is not None
    final = step + 1 == steps
    pieces = len(envs) - 1
    env = pltpu.VMEM((width, tile, tile), bf16)
    total = jax.ShapeDtypeStruct((2, width, tile, tile), bf16)
    n = width * GROUP
    scratch = [
        pltpu.VMEM((tile, 3 * tile), bf16),
        pltpu.VMEM((tile, tile), bf16),
        pltpu.VMEM((tile, tile), bf16),
        pltpu.VMEM((tile, 3 * tile), bf16),
        *[pltpu.VMEM(shape, bf16) for _ in range(2) for shape in ((4, n, 2 * tile), (2, 2 * n, 2 * tile))],
        pltpu.VMEM((4, width, tile, tile), bf16),
        pltpu.VMEM((2, width, tile, tile), bf16),
        pltpu.VMEM((4, tile, tile), bf16),
        pltpu.VMEM((4, tile, tile), bf16),
        pltpu.VMEM((n, n), bf16),
        pltpu.VMEM((2 * n, 2 * n), bf16),
        pltpu.SemaphoreType.DMA((2, 3)),
        pltpu.SemaphoreType.DMA((4,)),
    ]
    if not last:
        scratch += [pltpu.VMEM((width, tile, tile), bf16)] * 2 + [pltpu.SemaphoreType.DMA((2, 3))]
    operands = [in_vmem(b) if last else b for b in envs] + [*tensors, in_hbm(small), in_hbm(large)]
    info_shape = jax.ShapeDtypeStruct(info.shape, info.dtype)
    out_specs, out_shape = [ANY, SMEM], [total, info_shape]
    aliases = {}
    if last:
        operands.append(acc)
        out_specs, out_shape = [VMEM, SMEM], [env, info_shape]
        if final or not left:
            out_specs.insert(0, VMEM)
            out_shape.insert(0, env)
        if not final:
            out_specs.insert(0, VMEM)
            out_shape.insert(0, pltpu.VMEM((2 * width, tile, tile), bf16))
        if left:
            if onto is not None:
                operands.append(onto)
                aliases = {1 + len(operands): 0}
            out_specs.insert(0, ANY)
            out_shape.insert(0, jax.ShapeDtypeStruct((steps, 1, width, tile, tile), bf16))
            scratch.append(pltpu.SemaphoreType.DMA((3,)))

    def body(info, table, *refs):
        refs = (refs[0], refs[1 : 1 + pieces]) + refs[1 + pieces :]
        terms_body(left, last, final, onto is not None, width, tile, step, steps, info, table, *refs)

    return pl.pallas_call(
        body,
        in_specs=[SMEM, SMEM] + [VMEM if last else ANY] * len(envs) + [ANY] * (len(operands) - len(envs)),
        out_specs=out_specs,
        out_shape=out_shape,
        scratch_shapes=scratch,
        input_output_aliases=aliases,
        compiler_params=pltpu.CompilerParams(vmem_limit_bytes=LIMIT),
    )(info, table, *operands)


def place_body(groups, count, direct, info, *refs):
    pieces = 3
    total = sum(len(sources) for _, _, sources in groups)
    sources, outs, held, sem = refs[:total], refs[-2 - count : -2], refs[-2], refs[-1]
    jobs = []
    for n, (out, index, flags) in enumerate(groups):
        dst = outs[out] if index is None else outs[out].at[index, 0]
        for flag in flags:
            src = sources[len(jobs)]
            cuts = [src.shape[0] * k // pieces for k in range(pieces + 1)]
            spans = [pl.ds(a, b - a) for a, b in zip(cuts, cuts[1:])]
            here = held.at[n]
            reads = [pltpu.make_async_copy(src.at[c], here.at[c], sem.at[0, n, k]) for k, c in enumerate(spans)]
            writes = [pltpu.make_async_copy(here.at[c], dst.at[c], sem.at[1, n, k]) for k, c in enumerate(spans)]
            if direct[len(jobs)]:
                reads, writes = [pltpu.make_async_copy(src.at[c], dst.at[c], sem.at[1, n, k]) for k, c in enumerate(spans)], None
            jobs.append((flag, reads, writes))

    for flag, reads, _ in jobs:

        @pl.when(flag(info))
        def _(reads=reads):
            for c in reads:
                c.start()

    for flag, reads, writes in jobs:

        @pl.when(flag(info))
        def _(reads=reads, writes=writes):
            for a, b in zip(reads, writes or ()):
                a.wait()
                b.start()

    for flag, reads, writes in jobs:

        @pl.when(flag(info))
        def _(reads=reads, writes=writes):
            for c in writes or reads:
                c.wait()


def place(info, groups, shapes, onto, resident=()):
    sources = [b for _, _, pairs in groups for _, b in pairs]
    specs = [VMEM if any(b is r for r in resident) else ANY for b in sources]
    sources = [in_vmem(b) if spec is VMEM else b for b, spec in zip(sources, specs)]
    plan = [(out, index, [flag for flag, _ in pairs]) for out, index, pairs in groups]
    return pl.pallas_call(
        functools.partial(place_body, plan, len(shapes), [spec is VMEM for spec in specs]),
        in_specs=[SMEM] + specs + [ANY] * len(onto),
        out_specs=[ANY] * len(shapes),
        out_shape=[jax.ShapeDtypeStruct(s, bf16) for s in shapes],
        scratch_shapes=[
            pltpu.VMEM((len(groups), *sources[0].shape), bf16),
            pltpu.SemaphoreType.DMA((2, len(groups), 3)),
        ],
        compiler_params=pltpu.CompilerParams(vmem_limit_bytes=LIMIT),
        input_output_aliases={1 + len(sources) + i: i for i in range(len(onto))},
    )(info, *sources, *onto)


def compact(mpo):
    sites, width = mpo.shape[:2]
    return jnp.transpose(mpo, (0, 3, 2, 4, 1)).reshape(sites, 4 * width, 4 * width)


def shards(site_tensors, mpo, left_in, right_in, tile_rows):
    chains, sectors = lax.axis_size("chain"), lax.axis_size("sector")
    routes = Routes(chains, sectors)
    chain, sector = lax.axis_index("chain"), lax.axis_index("sector")
    core, x = chain % 2, sector % 2
    sites, _, tile = site_tensors.shape[:3]
    same = core == x
    info = jnp.stack([(chain - core + x) * sites, sector // 2, x, same.astype(jnp.int32), chain]).astype(jnp.int32)

    left_near, right_own = left_in[0, 0], right_in[0, 0]
    width = left_near.shape[0]
    tensors = jnp.transpose(site_tensors[:, 0], (0, 2, 1, 3)).reshape(sites * 4, tile, tile)
    packed = jnp.concatenate([left_near, tensors])
    left_cross = move(packed, routes.left_cross)
    left_second, right_own, tensors, packed = lax.optimization_barrier((left_near, right_own, tensors, packed))
    left_near_below = move(left_second, routes.left_up)
    right_near_above = move(right_own, routes.right_native_down)
    right_near = move(right_own, routes.to_right_core)
    tensors_below = move(tensors, routes.left_up)
    tensors_right = move(tensors, routes.to_right_core)
    k = compact(mpo)
    k_right = move(k, routes.to_right_core)
    right_own, k_right = lax.optimization_barrier((right_own, k_right))
    cuts = [0, width // 2, width] if width % 2 == 0 else [0, width]
    right_cross = [move(right_own[a:b], routes.right_cross) for a, b in zip(cuts, cuts[1:])]
    ks = spread(info, k, k_right)
    left_cross, left_near_below, right_near_above, ks, tensors_below, tensors_right = lax.optimization_barrier(
        (left_cross, left_near_below, right_near_above, ks, tensors_below, tensors_right)
    )
    left_cross_below = move(left_cross, routes.left_up)
    tensors_cross_right = move(left_cross[width:], routes.to_right_core)
    right_cross_above = [move(b, routes.right_down) for b in right_cross]
    pair, pair_below = (tensors, left_cross), (tensors_below, left_cross_below)
    pair_right = (tensors_right, tensors_cross_right)

    l_far, r_far = (left_near_below, left_cross_below), (right_near_above, *right_cross_above)
    l, r = (in_hbm(left_near), left_cross), (right_near, *right_cross)

    def local(left, step, info, envs, tensors):
        return terms(left, step, sites, info, tile_rows, envs, tensors, ks[3 * step], ks[3 * step + 1])

    def remote(left, step, info, envs, tensors, acc, onto=None):
        return terms(left, step, sites, info, tile_rows, envs, tensors, ks[3 * step + 2], ks[3 * step + 1], acc, onto)

    envs_shape = (sites, 1, width, tile, tile)

    def own(info):
        return info[3] == 1

    def other(info):
        return info[3] != 1

    left_envs = right_envs = None
    kept = []
    info, tensors_cross_right = lax.optimization_barrier((info, tensors_cross_right))
    pair_right = (tensors_right, tensors_cross_right)
    l_acc, info = local(True, 0, info, l, pair)
    for step in range(sites):
        more = step + 1 < sites
        if step > 0:
            kept.append((step, left_back, list(right_back)))
        left_envs, l_first, l_cross, info = remote(True, step, info, l_far, pair_below, l_acc, left_envs)
        left_back = move(l_cross, routes.left_back)
        if more:
            l_far = [move(l_first, routes.left_up)]
            l_acc, info = local(True, step + 1, info, [l_first], pair)
        if step == 0:
            r_acc, info = local(False, step, info, r, pair_right)
        if step > 0:
            info, *kept[-1][2][:] = lax.optimization_barrier((info, *kept[-1][2]))
        *r_pair, r_near, r_cross, info = remote(False, step, info, r_far, pair_right, r_acc)
        if more:
            r_far = [move(r_pair[0], routes.right_down)]
            info, left_back = lax.optimization_barrier((info, left_back))
        right_back = (move(r_near, routes.from_right_core), move(r_cross, routes.right_back))
        if more:
            r_acc, info = local(False, step + 1, info, r_pair, pair_right)
    info, left_back = lax.optimization_barrier((info, left_back))
    for step, back, backs in kept:
        left_envs, right_envs = place(
            info,
            [(0, step - 1, [(other, back)]), (1, sites - step, list(zip((own, other), backs)))],
            [envs_shape] * 2,
            [left_envs] + ([] if right_envs is None else [right_envs]),
        )

    edge_tile = move(jnp.where(same, l_first, left_back), routes.edge_same + routes.edge_other)
    edge = [
        (lambda info: info[4] == 0, left_in[0, 0]),
        (lambda info: info[4] != 0, edge_tile),
    ]
    left_envs, right_envs, left_edge = place(
        info,
        [(0, sites - 1, [(other, left_back)]), (1, 0, list(zip((own, other), right_back))), (2, None, edge)],
        [envs_shape, envs_shape, (width, tile, tile)],
        [left_envs] + ([] if right_envs is None else [right_envs]),
        [left_back, *right_back, edge_tile],
    )
    return left_envs, right_envs, left_edge[None, None]


def solution(mesh):
    placed = (
        P("chain", "sector", None, None, None),
        P("chain", None, None, None, None),
        P("chain", "sector", None, None, None),
        P("chain", "sector", None, None, None),
        P(),
    )
    return jax.shard_map(
        shards,
        mesh=mesh,
        in_specs=placed,
        out_specs=(
            P("chain", "sector", None, None, None),
            P("chain", "sector", None, None, None),
            P("chain", "sector", None, None, None),
        ),
        check_vma=False,
    )
```

profile of v0, /device:TPU:22, one launch (start us, length us, event | category | flops | bytes accessed | tf_op | source)
XLA Modules:
  0.0 149.9 jit_solution(17123943500366173684)
XLA Ops:
  0.6 1.0 copy.12
  1.6 2.8 %pad_maximum_fusion = bf16[50,128,128]{2,1,0:T(8,128)(2,1)} fusion(bf16[8,128,128]{2,1,0:T(8,128)(2,1)S(1)} %bitcast.17, bf16[42,128,128]{2,1,0:T(8,128)(2,1)} %bitcast.13), kind=kLoop, calls=%fused_computation | loop fusion | flops 819200 | bytes 3276800 | tf_op jit(solution)/shard_map/concatenate | solution.py:462
  4.4 2.7 %collective-permute-start = (bf16[50,128,128]{2,1,0:T(8,128)(2,1)}, bf16[50,128,128]{2,1,0:T(8,128)(2,1)S(1)}, u32[]{:S(2)}, u32[]{:S(2)}) collective-permute-start(bf16[50,128,128]{2,1,0:T(8,128)(2,1)} %pad_maximum_fusion), channel_id=1, source_target_pairs={{1,0},{8,9},{3,2},{10,11},{5,4},{12,13},{7,6},{14,15},{17,16},{24,... | collective-permute-start | bytes 4915208 | tf_op jit(solution)/shard_map/ppermute | solution.py:45
  7.1 1.8 %collective-permute-start.1 = (bf16[42,128,128]{2,1,0:T(8,128)(2,1)S(1)}, bf16[42,128,128]{2,1,0:T(8,128)(2,1)}, u32[]{:S(2)}, u32[]{:S(2)}) collective-permute-start(bf16[42,128,128]{2,1,0:T(8,128)(2,1)S(1)} %bitcast.15), channel_id=1, source_target_pairs={{0,2},{9,11},{2,4},{11,13},{4,6},{13,15},{16,18},{25,27},{18,20},{... | collective-permute-start | bytes 4128776 | tf_op jit(solution)/shard_map/ppermute | solution.py:45
  8.8 1.3 collective-permute-start.2
  10.1 2.1 %copy.13 = bf16[2,4,42,4,42]{4,3,2,1,0:T(4,128)(2,1)} copy(bf16[2,4,42,4,42]{2,3,1,4,0:T(4,128)(2,1)} %bitcast.22) | data formatting | bytes 225792 | tf_op jit(solution)/shard_map/transpose | solution.py:447
  12.3 1.9 %reshape.13.own = bf16[2,168,168]{2,1,0:T(8,128)(2,1)} reshape(bf16[2,4,42,4,42]{4,3,2,1,0:T(4,128)(2,1)} %copy.13) | data formatting | bytes 225792 | tf_op jit(solution)/shard_map/reshape | solution.py:447
  14.2 1.3 collective-permute-start.3
  15.5 1.3 collective-permute-start.5
  16.8 2.1 %collective-permute-done.3.received = bf16[2,168,168]{2,1,0:T(8,128)(2,1)S(1)} collective-permute-done((bf16[2,168,168]{2,1,0:T(8,128)(2,1)}, bf16[2,168,168]{2,1,0:T(8,128)(2,1)S(1)}, u32[]{:S(2)}, u32[]{:S(2)}) %collective-permute-start.3) | collective-permute-done | bytes 112928 | tf_op jit(solution)/shard_map/ppermute | solution.py:45
  18.9 0.7 copy-done.4
  19.5 1.4 collective-permute-start.4
  21.0 0.9 copy-done.5
  21.9 4.1 %shard_map.76 = (bf16[168,168]{1,0:T(8,128)(2,1)}, bf16[336,336]{1,0:T(8,128)(2,1)}, bf16[168,168]{1,0:T(8,128)(2,1)}, bf16[168,168]{1,0:T(8,128)(2,1)}, bf16[33...) custom-call(s32[5]{0:T(128)S(1)} %stack.27.info, bf16[2,168,168]{2,1,0:T(8,128)(2,1)} %reshape.13.own, ...), custom_call_target="tpu_custom_call" | custom-call | tf_op jit(solution)/shard_map/pallas_call | solution.py:105
  26.0 2.8 %collective-permute-done.2.refs_0_ = bf16[42,128,128]{2,1,0:T(8,128)(2,1)} collective-permute-done((bf16[42,128,128]{2,1,0:T(8,128)(2,1)}, bf16[42,128,128]{2,1,0:T(8,128)(2,1)}, u32[]{:S(2)}, u32[]{:S(2)}) %collective-permute-start.2) | collective-permute-done | bytes 1376288 | tf_op jit(solution)/shard_map/ppermute | solution.py:45
  28.8 0.8 collective-permute-start.7
  29.6 1.3 collective-permute-start.8
  31.0 1.4 collective-permute-start.6
  32.4 1.5 fusion
  33.9 2.6 %collective-permute-start.10 = (bf16[21,128,128]{2,1,0:T(8,128)(2,1)S(1)}, bf16[21,128,128]{2,1,0:T(8,128)(2,1)S(1)}, u32[]{:S(2)}, u32[]{:S(2)}) collective-permute-start(bf16[21,128,128]{2,1,0:T(8,128)(2,1)S(1)} %get-tuple-element.121), channel_id=1, source_target_pairs={{1,8},{8,1},{3,10},{10,3},{5,12},{12,5},{7,14},{14,7},{17,24},{24,... | collective-permute-start | bytes 2064392 | tf_op jit(solution)/shard_map/ppermute | solution.py:45
  36.4 3.0 %collective-permute-start.9 = (bf16[21,128,128]{2,1,0:T(8,128)(2,1)S(1)}, bf16[21,128,128]{2,1,0:T(8,128)(2,1)S(1)}, u32[]{:S(2)}, u32[]{:S(2)}) collective-permute-start(bf16[21,128,128]{2,1,0:T(8,128)(2,1)S(1)} %get-tuple-element.122), channel_id=1, source_target_pairs={{1,8},{8,1},{3,10},{10,3},{5,12},{12,5},{7,14},{14,7},{17,24},{24,... | collective-permute-start | bytes 2064392 | tf_op jit(solution)/shard_map/ppermute | solution.py:45
  39.5 1.4 shard_map.77
  40.9 2.1 %shard_map.78 = (bf16[2,1,42,128,128]{4,3,2,1,0:T(8,128)(2,1)}, bf16[84,128,128]{2,1,0:T(8,128)(2,1)S(1)}, bf16[42,128,128]{2,1,0:T(8,128)(2,1)S(1)}, s32[5]{0:T(128)S(1)}) custom-call(s32[5]{0:T(128)S(1)} %get-tuple-element.76.info, s32[9,8]{1,0:T(8,128)S(1)} %copy.14.table, bf16[42,128,128]{2,1,0:T(8,128)(2,1)} %collective-permute-done.1.refs_0_, ...), custom_call_target="tpu_custom_call" | custom-call | tf_op jit(solution)/shard_map/pallas_call | solution.py:374
  43.0 0.8 collective-permute-start.14
  43.8 2.3 %collective-permute-done.10.refs_2_ = bf16[21,128,128]{2,1,0:T(8,128)(2,1)S(1)} collective-permute-done((bf16[21,128,128]{2,1,0:T(8,128)(2,1)S(1)}, bf16[21,128,128]{2,1,0:T(8,128)(2,1)S(1)}, u32[]{:S(2)}, u32[]{:S(2)}) %collective-permute-start.10) | collective-permute-done | bytes 688160 | tf_op jit(solution)/shard_map/ppermute | solution.py:45
  46.1 2.3 %collective-permute-start.12 = (bf16[21,128,128]{2,1,0:T(8,128)(2,1)S(1)}, bf16[21,128,128]{2,1,0:T(8,128)(2,1)S(1)}, u32[]{:S(2)}, u32[]{:S(2)}) collective-permute-start(bf16[21,128,128]{2,1,0:T(8,128)(2,1)S(1)} %collective-permute-done.10.refs_2_), channel_id=1, source_target_pairs={{10,8},{3,1},{12,10},{5,3},{14,12},{7,5},{26,24},{19,17},{28,26},{... | collective-permute-start | bytes 2064392 | tf_op jit(solution)/shard_map/ppermute | solution.py:45
  48.5 5.0 %collective-permute-done.9.refs_1_ = bf16[21,128,128]{2,1,0:T(8,128)(2,1)S(1)} collective-permute-done((bf16[21,128,128]{2,1,0:T(8,128)(2,1)S(1)}, bf16[21,128,128]{2,1,0:T(8,128)(2,1)S(1)}, u32[]{:S(2)}, u32[]{:S(2)}) %collective-permute-start.9) | collective-permute-done | bytes 688160 | tf_op jit(solution)/shard_map/ppermute | solution.py:45
  53.5 2.3 %collective-permute-start.11 = (bf16[21,128,128]{2,1,0:T(8,128)(2,1)S(1)}, bf16[21,128,128]{2,1,0:T(8,128)(2,1)S(1)}, u32[]{:S(2)}, u32[]{:S(2)}) collective-permute-start(bf16[21,128,128]{2,1,0:T(8,128)(2,1)S(1)} %collective-permute-done.9.refs_1_), channel_id=1, source_target_pairs={{10,8},{3,1},{12,10},{5,3},{14,12},{7,5},{26,24},{19,17},{28,26},{... | collective-permute-start | bytes 2064392 | tf_op jit(solution)/shard_map/ppermute | solution.py:45
  55.9 1.3 collective-permute-start.13
  57.2 1.6 %shard_map.79 = (bf16[2,42,128,128]{3,2,1,0:T(8,128)(2,1)S(1)}, s32[5]{0:T(128)S(1)}) custom-call(s32[5]{0:T(128)S(1)} %get-tuple-element.81.info, s32[9,8]{1,0:T(8,128)S(1)} %copy.14.table, bf16[84,128,128]{2,1,0:T(8,128)(2,1)S(1)} %get-tuple-element.82.refs_0_, bf16[8,128,128]{2,1,0:T(8,128)(2,1)S(1)} %bitcast.21, ...), custom_call_target="tpu_custom_call" | custom-call | tf_op jit(solution)/shard_map/pallas_call | solution.py:374
  58.8 10.9 %shard_map.80 = (bf16[2,42,128,128]{3,2,1,0:T(8,128)(2,1)S(1)}, s32[5]{0:T(128)S(1)}) custom-call(s32[5]{0:T(128)S(1)} %get-tuple-element.85.info, s32[9,8]{1,0:T(8,128)S(1)} %copy.14.table, bf16[42,128,128]{2,1,0:T(8,128)(2,1)} %collective-permute-done.8.refs_0_, bf16[21,128,128]{2,1,0:T(8,128)(2,1)S(1)} %collective-permute-done.9.refs_1_, ...), custom_call_target="tpu_custom_call" | custom-call | tf_op jit(solution)/shard_map/pallas_call | solution.py:374
  69.7 10.0 %shard_map.81 = (bf16[84,128,128]{2,1,0:T(8,128)(2,1)S(1)}, bf16[42,128,128]{2,1,0:T(8,128)(2,1)S(1)}, bf16[42,128,128]{2,1,0:T(8,128)(2,1)S(1)}, s32[5]{0:T(128)S(1)}) custom-call(s32[5]{0:T(128)S(1)} %get-tuple-element.89.info, s32[9,8]{1,0:T(8,128)S(1)} %copy.14.table, bf16[42,128,128]{2,1,0:T(8,128)(2,1)} %collective-permute-done.2.refs_0_, ...), custom_call_target="tpu_custom_call" | custom-call | tf_op jit(solution)/shard_map/pallas_call | solution.py:374
  79.7 2.4 %collective-permute-start.17 = (bf16[84,128,128]{2,1,0:T(8,128)(2,1)S(1)}, bf16[84,128,128]{2,1,0:T(8,128)(2,1)S(1)}, u32[]{:S(2)}, u32[]{:S(2)}) collective-permute-start(bf16[84,128,128]{2,1,0:T(8,128)(2,1)S(1)} %get-tuple-element.95.refs_0_), channel_id=1, source_target_pairs={{10,8},{3,1},{12,10},{5,3},{14,12},{7,5},{26,24},{19,17},{28,26},{... | collective-permute-start | bytes 8257544 | tf_op jit(solution)/shard_map/ppermute | solution.py:45
  82.0 2.8 %collective-permute-start.15 = (bf16[42,128,128]{2,1,0:T(8,128)(2,1)S(1)}, bf16[42,128,128]{2,1,0:T(8,128)(2,1)S(1)}, u32[]{:S(2)}, u32[]{:S(2)}) collective-permute-start(bf16[42,128,128]{2,1,0:T(8,128)(2,1)S(1)} %get-tuple-element.101), channel_id=1, source_target_pairs={{8,0},{1,9},{10,2},{3,11},{12,4},{5,13},{14,6},{7,15},{24,16},{17,... | collective-permute-start | bytes 4128776 | tf_op jit(solution)/shard_map/ppermute | solution.py:45
  84.8 5.0 %collective-permute-start.16 = (bf16[42,128,128]{2,1,0:T(8,128)(2,1)S(1)}, bf16[42,128,128]{2,1,0:T(8,128)(2,1)S(1)}, u32[]{:S(2)}, u32[]{:S(2)}) collective-permute-start(bf16[42,128,128]{2,1,0:T(8,128)(2,1)S(1)} %get-tuple-element.102), channel_id=1, source_target_pairs={{8,1},{1,8},{10,3},{3,10},{12,5},{5,12},{14,7},{7,14},{24,17},{17,... | collective-permute-start | bytes 4128776 | tf_op jit(solution)/shard_map/ppermute | solution.py:45
  89.8 12.1 %shard_map.82 = (bf16[2,42,128,128]{3,2,1,0:T(8,128)(2,1)S(1)}, s32[5]{0:T(128)S(1)}) custom-call(s32[5]{0:T(128)S(1)} %get-tuple-element.94.info, s32[9,8]{1,0:T(8,128)S(1)} %copy.14.table, bf16[84,128,128]{2,1,0:T(8,128)(2,1)S(1)} %get-tuple-element.95.refs_0_, bf16[8,128,128]{2,1,0:T(8,128)(2,1)S(1)} %collective-permute-done.5.refs_3_.refs_1_, ...), custom_call_target="tpu_custom_call" | custom-call | tf_op jit(solution)/shard_map/pallas_call | solution.py:374
  101.9 1.4 shard_map.83
  103.3 1.3 collective-permute-start.18
  104.6 1.2 collective-permute-done.16.refs_2_
  105.8 8.8 %collective-permute-done.17.refs_0_ = bf16[84,128,128]{2,1,0:T(8,128)(2,1)S(1)} collective-permute-done((bf16[84,128,128]{2,1,0:T(8,128)(2,1)S(1)}, bf16[84,128,128]{2,1,0:T(8,128)(2,1)S(1)}, u32[]{:S(2)}, u32[]{:S(2)}) %collective-permute-start.17) | collective-permute-done | bytes 2752544 | tf_op jit(solution)/shard_map/ppermute | solution.py:45
  114.6 9.3 %shard_map.84 = (bf16[42,128,128]{2,1,0:T(8,128)(2,1)S(1)}, bf16[42,128,128]{2,1,0:T(8,128)(2,1)S(1)}, s32[5]{0:T(128)S(1)}) custom-call(s32[5]{0:T(128)S(1)} %get-tuple-element.103.info, s32[9,8]{1,0:T(8,128)S(1)} %copy.14.table, bf16[84,128,128]{2,1,0:T(8,128)(2,1)S(1)} %collective-permute-done.17.refs_0_, ...), custom_call_target="tpu_custom_call" | custom-call | tf_op jit(solution)/shard_map/pallas_call | solution.py:374
  123.9 1.4 collective-permute-start.19
  125.3 1.9 %collective-permute-start.20 = (bf16[42,128,128]{2,1,0:T(8,128)(2,1)S(1)}, bf16[42,128,128]{2,1,0:T(8,128)(2,1)S(1)}, u32[]{:S(2)}, u32[]{:S(2)}) collective-permute-start(bf16[42,128,128]{2,1,0:T(8,128)(2,1)S(1)} %get-tuple-element.110), channel_id=1, source_target_pairs={{8,1},{1,8},{10,3},{3,10},{12,5},{5,12},{14,7},{7,14},{24,17},{17,... | collective-permute-start | bytes 4128776 | tf_op jit(solution)/shard_map/ppermute | solution.py:45
  127.4 1.9 %collective-permute-start.21 = (bf16[42,128,128]{2,1,0:T(8,128)(2,1)S(1)}, bf16[42,128,128]{2,1,0:T(8,128)(2,1)S(1)}, u32[]{:S(2)}, u32[]{:S(2)}) collective-permute-start(bf16[42,128,128]{2,1,0:T(8,128)(2,1)S(1)} %broadcast_select_fusion), channel_id=1, source_target_pairs={{0,8},{2,10},{4,12},{6,14},{9,17},{11,19},{13,21},{15,23},{16,24},... | collective-permute-start | bytes 4128776 | tf_op jit(solution)/shard_map/ppermute | solution.py:45
  129.3 3.8 %shard_map.85 = (bf16[2,1,42,128,128]{4,3,2,1,0:T(8,128)(2,1)}, bf16[2,1,42,128,128]{4,3,2,1,0:T(8,128)(2,1)}) custom-call(s32[5]{0:T(128)S(1)} %get-tuple-element.107.info, bf16[42,128,128]{2,1,0:T(8,128)(2,1)S(1)} %collective-permute-done.13.refs_0_, bf16[42,128,128]{2,1,0:T(8,128)(2,1)S(1)} %collective-permute-done.15.refs_1_, ...), custom_call_target="tpu_custom_call", output_to_operand_aliasing={{0}: (4, {})} | custom-call | tf_op jit(solution)/shard_map/pallas_call | solution.py:431
  133.1 11.8 %collective-permute-done.20.refs_2_ = bf16[42,128,128]{2,1,0:T(8,128)(2,1)S(1)} collective-permute-done((bf16[42,128,128]{2,1,0:T(8,128)(2,1)S(1)}, bf16[42,128,128]{2,1,0:T(8,128)(2,1)S(1)}, u32[]{:S(2)}, u32[]{:S(2)}) %collective-permute-start.20) | collective-permute-done | bytes 1376288 | tf_op jit(solution)/shard_map/ppermute | solution.py:45
  144.9 2.1 %collective-permute-done.21.refs_4_ = bf16[42,128,128]{2,1,0:T(8,128)(2,1)S(1)} collective-permute-done((bf16[42,128,128]{2,1,0:T(8,128)(2,1)S(1)}, bf16[42,128,128]{2,1,0:T(8,128)(2,1)S(1)}, u32[]{:S(2)}, u32[]{:S(2)}) %collective-permute-start.21) | collective-permute-done | bytes 1376288 | tf_op jit(solution)/shard_map/ppermute | solution.py:45
  147.0 2.7 %shard_map.86 = (bf16[2,1,42,128,128]{4,3,2,1,0:T(8,128)(2,1)}, bf16[2,1,42,128,128]{4,3,2,1,0:T(8,128)(2,1)}, bf16[42,128,128]{2,1,0:T(8,128)(2,1)}) custom-call(s32[5]{0:T(128)S(1)} %get-tuple-element.107.info, bf16[42,128,128]{2,1,0:T(8,128)(2,1)S(1)} %collective-permute-done.18.refs_0_, ...), custom_call_target="tpu_custom_call", output_to_operand_aliasing={{0}: (6, {}), {1}: (7, {})} | custom-call | tf_op jit(solution)/shard_map/pallas_call | solution.py:431
  (30 shorter events, 0.4 us)
Async XLA Ops:
  1.6 17.2 %copy-start.2 = (bf16[2,4,128,128]{3,2,1,0:T(8,128)(2,1)}, bf16[2,4,128,128]{3,2,1,0:T(8,128)(2,1)S(1)}, u32[]{:S(2)}) copy-start(bf16[2,4,128,128]{3,2,1,0:T(8,128)(2,1)S(1)} %copy.12) | copy-start | bytes 786436
  1.6 5.5 %copy-start = (bf16[1,1,42,128,128]{4,3,2,1,0:T(8,128)(2,1)S(1)}, bf16[1,1,42,128,128]{4,3,2,1,0:T(8,128)(2,1)}, u32[]{:S(2)}) copy-start(bf16[1,1,42,128,128]{4,3,2,1,0:T(8,128)(2,1)} %param.7) | copy-start | bytes 4128772
  4.4 26.4 %copy-start.6 = (s32[9,8]{0,1:T(8,128)S(1)}, s32[9,8]{0,1:T(8,128)}, u32[]{:S(2)}) copy-start(s32[9,8]{0,1:T(8,128)} %param.9) | copy-start | bytes 868
  4.4 24.4 %collective-permute-start = (bf16[50,128,128]{2,1,0:T(8,128)(2,1)}, bf16[50,128,128]{2,1,0:T(8,128)(2,1)S(1)}, u32[]{:S(2)}, u32[]{:S(2)}) collective-permute-start(bf16[50,128,128]{2,1,0:T(8,128)(2,1)} %pad_maximum_fusion), channel_id=1, source_target_pairs={{1,0},{8,9},{3,2},{10,11},{5,4},{12,13},{7,6},{14,15},{17,16},{24,... | collective-permute-start | bytes 4915208 | tf_op jit(solution)/shard_map/ppermute | solution.py:45
  7.1 18.9 %collective-permute-start.1 = (bf16[42,128,128]{2,1,0:T(8,128)(2,1)S(1)}, bf16[42,128,128]{2,1,0:T(8,128)(2,1)}, u32[]{:S(2)}, u32[]{:S(2)}) collective-permute-start(bf16[42,128,128]{2,1,0:T(8,128)(2,1)S(1)} %bitcast.15), channel_id=1, source_target_pairs={{0,2},{9,11},{2,4},{11,13},{4,6},{13,15},{16,18},{25,27},{18,20},{... | collective-permute-start | bytes 4128776 | tf_op jit(solution)/shard_map/ppermute | solution.py:45
  8.8 19.9 %collective-permute-start.2 = (bf16[42,128,128]{2,1,0:T(8,128)(2,1)}, bf16[42,128,128]{2,1,0:T(8,128)(2,1)}, u32[]{:S(2)}, u32[]{:S(2)}) collective-permute-start(bf16[42,128,128]{2,1,0:T(8,128)(2,1)} %bitcast.9), channel_id=1, source_target_pairs={{2,8},{11,1},{4,10},{13,3},{6,12},{15,5},{18,24},{27,17},{20,26},{... | collective-permute-start | bytes 4128776 | tf_op jit(solution)/shard_map/ppermute | solution.py:45
  14.2 4.7 %collective-permute-start.3 = (bf16[2,168,168]{2,1,0:T(8,128)(2,1)}, bf16[2,168,168]{2,1,0:T(8,128)(2,1)S(1)}, u32[]{:S(2)}, u32[]{:S(2)}) collective-permute-start(bf16[2,168,168]{2,1,0:T(8,128)(2,1)} %reshape.13.own), channel_id=1, source_target_pairs={{0,8},{9,1},{2,10},{11,3},{4,12},{13,5},{6,14},{15,7},{16,24},{25,... | collective-permute-start | bytes 338696 | tf_op jit(solution)/shard_map/ppermute | solution.py:45
  15.5 10.5 %collective-permute-start.5 = (bf16[8,128,128]{2,1,0:T(8,128)(2,1)S(1)}, bf16[8,128,128]{2,1,0:T(8,128)(2,1)S(1)}, u32[]{:S(2)}, u32[]{:S(2)}) collective-permute-start(bf16[8,128,128]{2,1,0:T(8,128)(2,1)S(1)} %bitcast.18), channel_id=1, source_target_pairs={{0,8},{9,1},{2,10},{11,3},{4,12},{13,5},{6,14},{15,7},{16,24},{25,... | collective-permute-start | bytes 786440 | tf_op jit(solution)/shard_map/ppermute | solution.py:45
  18.8 0.7 copy-start.4
  19.5 6.5 %collective-permute-start.4 = (bf16[8,128,128]{2,1,0:T(8,128)(2,1)S(1)}, bf16[8,128,128]{2,1,0:T(8,128)(2,1)}, u32[]{:S(2)}, u32[]{:S(2)}) collective-permute-start(bf16[8,128,128]{2,1,0:T(8,128)(2,1)S(1)} %bitcast.19), channel_id=1, source_target_pairs={{0,2},{9,11},{2,4},{11,13},{4,6},{13,15},{16,18},{25,27},{18,20},{... | collective-permute-start | bytes 786440 | tf_op jit(solution)/shard_map/ppermute | solution.py:45
  21.0 0.9 copy-start.5
  28.8 12.1 %collective-permute-start.7 = (bf16[50,128,128]{2,1,0:T(8,128)(2,1)S(1)}, bf16[50,128,128]{2,1,0:T(8,128)(2,1)S(1)}, u32[]{:S(2)}, u32[]{:S(2)}) collective-permute-start(bf16[50,128,128]{2,1,0:T(8,128)(2,1)S(1)} %collective-permute-done.refs_1_.refs_3_.refs_2_), channel_id=1, source_target_pairs={{0,2},{9,11},{2,4},{11,13},{4,6},{13,15},{16,18},{25,27},{18,20},{... | collective-permute-start | bytes 4915208 | tf_op jit(solution)/shard_map/ppermute | solution.py:45
  29.6 29.2 %collective-permute-start.8 = (bf16[42,128,128]{2,1,0:T(8,128)(2,1)}, bf16[42,128,128]{2,1,0:T(8,128)(2,1)}, u32[]{:S(2)}, u32[]{:S(2)}) collective-permute-start(bf16[42,128,128]{2,1,0:T(8,128)(2,1)} %bitcast.9), channel_id=1, source_target_pairs={{0,8},{9,1},{2,10},{11,3},{4,12},{13,5},{6,14},{15,7},{16,24},{25,... | collective-permute-start | bytes 4128776 | tf_op jit(solution)/shard_map/ppermute | solution.py:45
  31.0 8.5 %copy-start.3 = (bf16[2,4,128,128]{3,2,1,0:T(8,128)(2,1)S(1)}, bf16[2,4,128,128]{3,2,1,0:T(8,128)(2,1)}, u32[]{:S(2)}) copy-start(bf16[2,4,128,128]{3,2,1,0:T(8,128)(2,1)} %copy-done.2) | copy-start | bytes 786436
  31.0 8.5 %collective-permute-start.6 = (bf16[8,128,128]{2,1,0:T(8,128)(2,1)S(1)}, bf16[8,128,128]{2,1,0:T(8,128)(2,1)S(1)}, u32[]{:S(2)}, u32[]{:S(2)}) collective-permute-start(bf16[8,128,128]{2,1,0:T(8,128)(2,1)S(1)} %slice.9), channel_id=1, source_target_pairs={{0,8},{9,1},{2,10},{11,3},{4,12},{13,5},{6,14},{15,7},{16,24},{25,... | collective-permute-start | bytes 786440 | tf_op jit(solution)/shard_map/ppermute | solution.py:45
  33.9 12.3 %collective-permute-start.10 = (bf16[21,128,128]{2,1,0:T(8,128)(2,1)S(1)}, bf16[21,128,128]{2,1,0:T(8,128)(2,1)S(1)}, u32[]{:S(2)}, u32[]{:S(2)}) collective-permute-start(bf16[21,128,128]{2,1,0:T(8,128)(2,1)S(1)} %get-tuple-element.121), channel_id=1, source_target_pairs={{1,8},{8,1},{3,10},{10,3},{5,12},{12,5},{7,14},{14,7},{17,24},{24,... | collective-permute-start | bytes 2064392 | tf_op jit(solution)/shard_map/ppermute | solution.py:45
  36.4 17.1 %collective-permute-start.9 = (bf16[21,128,128]{2,1,0:T(8,128)(2,1)S(1)}, bf16[21,128,128]{2,1,0:T(8,128)(2,1)S(1)}, u32[]{:S(2)}, u32[]{:S(2)}) collective-permute-start(bf16[21,128,128]{2,1,0:T(8,128)(2,1)S(1)} %get-tuple-element.122), channel_id=1, source_target_pairs={{1,8},{8,1},{3,10},{10,3},{5,12},{12,5},{7,14},{14,7},{17,24},{24,... | collective-permute-start | bytes 2064392 | tf_op jit(solution)/shard_map/ppermute | solution.py:45
  43.0 58.9 %collective-permute-start.14 = (bf16[84,128,128]{2,1,0:T(8,128)(2,1)S(1)}, bf16[84,128,128]{2,1,0:T(8,128)(2,1)S(1)}, u32[]{:S(2)}, u32[]{:S(2)}) collective-permute-start(bf16[84,128,128]{2,1,0:T(8,128)(2,1)S(1)} %get-tuple-element.82.refs_0_), channel_id=1, source_target_pairs={{0,2},{9,11},{2,4},{11,13},{4,6},{13,15},{16,18},{25,27},{18,20},{... | collective-permute-start | bytes 8257544 | tf_op jit(solution)/shard_map/ppermute | solution.py:45
  46.1 23.5 %collective-permute-start.12 = (bf16[21,128,128]{2,1,0:T(8,128)(2,1)S(1)}, bf16[21,128,128]{2,1,0:T(8,128)(2,1)S(1)}, u32[]{:S(2)}, u32[]{:S(2)}) collective-permute-start(bf16[21,128,128]{2,1,0:T(8,128)(2,1)S(1)} %collective-permute-done.10.refs_2_), channel_id=1, source_target_pairs={{10,8},{3,1},{12,10},{5,3},{14,12},{7,5},{26,24},{19,17},{28,26},{... | collective-permute-start | bytes 2064392 | tf_op jit(solution)/shard_map/ppermute | solution.py:45
  53.5 16.2 %collective-permute-start.11 = (bf16[21,128,128]{2,1,0:T(8,128)(2,1)S(1)}, bf16[21,128,128]{2,1,0:T(8,128)(2,1)S(1)}, u32[]{:S(2)}, u32[]{:S(2)}) collective-permute-start(bf16[21,128,128]{2,1,0:T(8,128)(2,1)S(1)} %collective-permute-done.9.refs_1_), channel_id=1, source_target_pairs={{10,8},{3,1},{12,10},{5,3},{14,12},{7,5},{26,24},{19,17},{28,26},{... | collective-permute-start | bytes 2064392 | tf_op jit(solution)/shard_map/ppermute | solution.py:45
  55.9 34.0 %collective-permute-start.13 = (bf16[42,128,128]{2,1,0:T(8,128)(2,1)S(1)}, bf16[42,128,128]{2,1,0:T(8,128)(2,1)S(1)}, u32[]{:S(2)}, u32[]{:S(2)}) collective-permute-start(bf16[42,128,128]{2,1,0:T(8,128)(2,1)S(1)} %get-tuple-element.93), channel_id=1, source_target_pairs={{0,1},{9,8},{2,3},{11,10},{4,5},{13,12},{6,7},{15,14},{16,17},{25,... | collective-permute-start | bytes 4128776 | tf_op jit(solution)/shard_map/ppermute | solution.py:45
  79.7 35.0 %collective-permute-start.17 = (bf16[84,128,128]{2,1,0:T(8,128)(2,1)S(1)}, bf16[84,128,128]{2,1,0:T(8,128)(2,1)S(1)}, u32[]{:S(2)}, u32[]{:S(2)}) collective-permute-start(bf16[84,128,128]{2,1,0:T(8,128)(2,1)S(1)} %get-tuple-element.95.refs_0_), channel_id=1, source_target_pairs={{10,8},{3,1},{12,10},{5,3},{14,12},{7,5},{26,24},{19,17},{28,26},{... | collective-permute-start | bytes 8257544 | tf_op jit(solution)/shard_map/ppermute | solution.py:45
  82.0 22.6 %collective-permute-start.15 = (bf16[42,128,128]{2,1,0:T(8,128)(2,1)S(1)}, bf16[42,128,128]{2,1,0:T(8,128)(2,1)S(1)}, u32[]{:S(2)}, u32[]{:S(2)}) collective-permute-start(bf16[42,128,128]{2,1,0:T(8,128)(2,1)S(1)} %get-tuple-element.101), channel_id=1, source_target_pairs={{8,0},{1,9},{10,2},{3,11},{12,4},{5,13},{14,6},{7,15},{24,16},{17,... | collective-permute-start | bytes 4128776 | tf_op jit(solution)/shard_map/ppermute | solution.py:45
  84.8 21.0 %collective-permute-start.16 = (bf16[42,128,128]{2,1,0:T(8,128)(2,1)S(1)}, bf16[42,128,128]{2,1,0:T(8,128)(2,1)S(1)}, u32[]{:S(2)}, u32[]{:S(2)}) collective-permute-start(bf16[42,128,128]{2,1,0:T(8,128)(2,1)S(1)} %get-tuple-element.102), channel_id=1, source_target_pairs={{8,1},{1,8},{10,3},{3,10},{12,5},{5,12},{14,7},{7,14},{24,17},{17,... | collective-permute-start | bytes 4128776 | tf_op jit(solution)/shard_map/ppermute | solution.py:45
  103.3 23.9 %collective-permute-start.18 = (bf16[42,128,128]{2,1,0:T(8,128)(2,1)S(1)}, bf16[42,128,128]{2,1,0:T(8,128)(2,1)S(1)}, u32[]{:S(2)}, u32[]{:S(2)}) collective-permute-start(bf16[42,128,128]{2,1,0:T(8,128)(2,1)S(1)} %get-tuple-element.106), channel_id=1, source_target_pairs={{0,1},{9,8},{2,3},{11,10},{4,5},{13,12},{6,7},{15,14},{16,17},{25,... | collective-permute-start | bytes 4128776 | tf_op jit(solution)/shard_map/ppermute | solution.py:45
  123.9 9.2 %collective-permute-start.19 = (bf16[42,128,128]{2,1,0:T(8,128)(2,1)S(1)}, bf16[42,128,128]{2,1,0:T(8,128)(2,1)S(1)}, u32[]{:S(2)}, u32[]{:S(2)}) collective-permute-start(bf16[42,128,128]{2,1,0:T(8,128)(2,1)S(1)} %get-tuple-element.109), channel_id=1, source_target_pairs={{8,0},{1,9},{10,2},{3,11},{12,4},{5,13},{14,6},{7,15},{24,16},{17,... | collective-permute-start | bytes 4128776 | tf_op jit(solution)/shard_map/ppermute | solution.py:45
  125.3 19.6 %collective-permute-start.20 = (bf16[42,128,128]{2,1,0:T(8,128)(2,1)S(1)}, bf16[42,128,128]{2,1,0:T(8,128)(2,1)S(1)}, u32[]{:S(2)}, u32[]{:S(2)}) collective-permute-start(bf16[42,128,128]{2,1,0:T(8,128)(2,1)S(1)} %get-tuple-element.110), channel_id=1, source_target_pairs={{8,1},{1,8},{10,3},{3,10},{12,5},{5,12},{14,7},{7,14},{24,17},{17,... | collective-permute-start | bytes 4128776 | tf_op jit(solution)/shard_map/ppermute | solution.py:45
  127.4 19.6 %collective-permute-start.21 = (bf16[42,128,128]{2,1,0:T(8,128)(2,1)S(1)}, bf16[42,128,128]{2,1,0:T(8,128)(2,1)S(1)}, u32[]{:S(2)}, u32[]{:S(2)}) collective-permute-start(bf16[42,128,128]{2,1,0:T(8,128)(2,1)S(1)} %broadcast_select_fusion), channel_id=1, source_target_pairs={{0,8},{2,10},{4,12},{6,14},{9,17},{11,19},{13,21},{15,23},{16,24},... | collective-permute-start | bytes 4128776 | tf_op jit(solution)/shard_map/ppermute | solution.py:45
  129.3 17.7 %copy-start.1 = (bf16[1,1,42,128,128]{4,3,2,1,0:T(8,128)(2,1)S(1)}, bf16[1,1,42,128,128]{4,3,2,1,0:T(8,128)(2,1)}, u32[]{:S(2)}) copy-start(bf16[1,1,42,128,128]{4,3,2,1,0:T(8,128)(2,1)} %param.7) | copy-start | bytes 4128772
where the time goes:
time: 151 us; the launch traced here: 150 us
  Pallas kernels  59.3 us (39%)
  starting transfers between devices  42.2 us (28%)
  waiting for transfers between devices  36 us (24%)
  local copies, waits for them, and re-layouts  8.28 us (5%)
  other arithmetic  2.91 us (2%)
    pallas_call x8, Pallas kernels, terms(): pl.pallas_call(body, in_specs=[SMEM, SMEM] + [VMEM if last else ANY] * le...  48.7 us
    ppermute x22, starting transfers between devices, move(): return lax.ppermute(block, AXES, route)  42.2 us
    ppermute x22, waiting for transfers between devices, move(): return lax.ppermute(block, AXES, route)  36 us
    pallas_call x2, Pallas kernels, place(): pl.pallas_call(functools.partial(place_body, plan, len(shapes), [spec is...  6.49 us
    pallas_call x1, Pallas kernels, spread(): pl.pallas_call(functools.partial(spread_body, width, steps), in_specs=[SM...  4.08 us
  transfers between devices with their start and end apart: 22, of which 8 were waited for; matrix products, arithmetic and copies ran while one was open for 4% of the time, Pallas kernels for 38%

commit v1 on v0

--- a/solution.py
+++ b/solution.py
@@ -512,12 +512,13 @@
         left_back = move(l_cross, routes.left_back)
         if more:
             l_far = [move(l_first, routes.left_up)]
-            l_acc, info = local(True, step + 1, info, [l_first], pair)
         if step == 0:
             r_acc, info = local(False, step, info, r, pair_right)
         if step > 0:
             info, *kept[-1][2][:] = lax.optimization_barrier((info, *kept[-1][2]))
         *r_pair, r_near, r_cross, info = remote(False, step, info, r_far, pair_right, r_acc)
+        if more:
+            l_acc, info = local(True, step + 1, info, [l_first], pair)
         if more:
             r_far = [move(r_pair[0], routes.right_down)]
             info, left_back = lax.optimization_barrier((info, left_back))

time: 151 us -> 149 us (0.987)
  starting transfers between devices: 42.2 us -> 37.8 us
  waiting for transfers between devices: 36 us -> 39 us
    ppermute x22, starting transfers between devices: 42.2 us -> 37.8 us  [move(): return lax.ppermute(block, AXES, route)]
    ppermute x22, waiting for transfers between devices: 36 us -> 39 us  [move(): return lax.ppermute(block, AXES, route)]
  transfers between devices with their start and end apart: 22 -> 22, of which waited for: 8 -> 9; matrix products, arithmetic and copies ran while one was open for 4% -> 4% of each run, Pallas kernels for 38% -> 38%
where the time goes in v1:
time: 149 us; the launch traced here: 148 us
  Pallas kernels  59.3 us (40%)
  waiting for transfers between devices  39 us (26%)
  starting transfers between devices  37.8 us (25%)
  local copies, waits for them, and re-layouts  8.23 us (6%)
  other arithmetic  2.95 us (2%)
    pallas_call x8, Pallas kernels, terms(): pl.pallas_call(body, in_specs=[SMEM, SMEM] + [VMEM if last else ANY] * le...  48.7 us
    ppermute x22, waiting for transfers between devices, move(): return lax.ppermute(block, AXES, route)  39 us
    ppermute x22, starting transfers between devices, move(): return lax.ppermute(block, AXES, route)  37.8 us
    pallas_call x2, Pallas kernels, place(): pl.pallas_call(functools.partial(place_body, plan, len(shapes), [spec is...  6.49 us
    pallas_call x1, Pallas kernels, spread(): pl.pallas_call(functools.partial(spread_body, width, steps), in_specs=[SM...  4.08 us
  transfers between devices with their start and end apart: 22, of which 9 were waited for; matrix products, arithmetic and copies ran while one was open for 4% of the time, Pallas kernels for 38%

profile of v1, /device:TPU:22, one launch (start us, length us, event | category | flops | bytes accessed | tf_op | source)
XLA Modules:
  0.0 148.4 jit_solution(2012240718589907457)
XLA Ops:
  0.6 1.0 copy.12
  1.6 2.8 %pad_maximum_fusion = bf16[50,128,128]{2,1,0:T(8,128)(2,1)} fusion(bf16[8,128,128]{2,1,0:T(8,128)(2,1)S(1)} %bitcast.17, bf16[42,128,128]{2,1,0:T(8,128)(2,1)} %bitcast.13), kind=kLoop, calls=%fused_computation | loop fusion | flops 819200 | bytes 3276800 | tf_op jit(solution)/shard_map/concatenate | solution.py:462
  4.4 2.7 %collective-permute-start = (bf16[50,128,128]{2,1,0:T(8,128)(2,1)}, bf16[50,128,128]{2,1,0:T(8,128)(2,1)S(1)}, u32[]{:S(2)}, u32[]{:S(2)}) collective-permute-start(bf16[50,128,128]{2,1,0:T(8,128)(2,1)} %pad_maximum_fusion), channel_id=1, source_target_pairs={{1,0},{8,9},{3,2},{10,11},{5,4},{12,13},{7,6},{14,15},{17,16},{24,... | collective-permute-start | bytes 4915208 | tf_op jit(solution)/shard_map/ppermute | solution.py:45
  7.1 1.8 %collective-permute-start.1 = (bf16[42,128,128]{2,1,0:T(8,128)(2,1)S(1)}, bf16[42,128,128]{2,1,0:T(8,128)(2,1)}, u32[]{:S(2)}, u32[]{:S(2)}) collective-permute-start(bf16[42,128,128]{2,1,0:T(8,128)(2,1)S(1)} %bitcast.15), channel_id=1, source_target_pairs={{0,2},{9,11},{2,4},{11,13},{4,6},{13,15},{16,18},{25,27},{18,20},{... | collective-permute-start | bytes 4128776 | tf_op jit(solution)/shard_map/ppermute | solution.py:45
  8.8 1.3 collective-permute-start.2
  10.1 2.1 %copy.13 = bf16[2,4,42,4,42]{4,3,2,1,0:T(4,128)(2,1)} copy(bf16[2,4,42,4,42]{2,3,1,4,0:T(4,128)(2,1)} %bitcast.22) | data formatting | bytes 225792 | tf_op jit(solution)/shard_map/transpose | solution.py:447
  12.3 1.9 %reshape.13.own = bf16[2,168,168]{2,1,0:T(8,128)(2,1)} reshape(bf16[2,4,42,4,42]{4,3,2,1,0:T(4,128)(2,1)} %copy.13) | data formatting | bytes 225792 | tf_op jit(solution)/shard_map/reshape | solution.py:447
  14.2 1.3 collective-permute-start.3
  15.5 1.3 collective-permute-start.5
  16.8 2.1 %collective-permute-done.3.received = bf16[2,168,168]{2,1,0:T(8,128)(2,1)S(1)} collective-permute-done((bf16[2,168,168]{2,1,0:T(8,128)(2,1)}, bf16[2,168,168]{2,1,0:T(8,128)(2,1)S(1)}, u32[]{:S(2)}, u32[]{:S(2)}) %collective-permute-start.3) | collective-permute-done | bytes 112928 | tf_op jit(solution)/shard_map/ppermute | solution.py:45
  18.9 0.7 copy-done.4
  19.5 1.4 collective-permute-start.4
  21.0 0.9 copy-done.5
  21.9 4.1 %shard_map.76 = (bf16[168,168]{1,0:T(8,128)(2,1)}, bf16[336,336]{1,0:T(8,128)(2,1)}, bf16[168,168]{1,0:T(8,128)(2,1)}, bf16[168,168]{1,0:T(8,128)(2,1)}, bf16[33...) custom-call(s32[5]{0:T(128)S(1)} %stack.27.info, bf16[2,168,168]{2,1,0:T(8,128)(2,1)} %reshape.13.own, ...), custom_call_target="tpu_custom_call" | custom-call | tf_op jit(solution)/shard_map/pallas_call | solution.py:105
  26.0 2.8 %collective-permute-done.2.refs_0_ = bf16[42,128,128]{2,1,0:T(8,128)(2,1)} collective-permute-done((bf16[42,128,128]{2,1,0:T(8,128)(2,1)}, bf16[42,128,128]{2,1,0:T(8,128)(2,1)}, u32[]{:S(2)}, u32[]{:S(2)}) %collective-permute-start.2) | collective-permute-done | bytes 1376288 | tf_op jit(solution)/shard_map/ppermute | solution.py:45
  28.8 0.8 collective-permute-start.7
  29.6 1.3 collective-permute-start.8
  31.0 1.4 collective-permute-start.6
  32.4 1.4 fusion
  33.8 2.6 %collective-permute-start.10 = (bf16[21,128,128]{2,1,0:T(8,128)(2,1)S(1)}, bf16[21,128,128]{2,1,0:T(8,128)(2,1)S(1)}, u32[]{:S(2)}, u32[]{:S(2)}) collective-permute-start(bf16[21,128,128]{2,1,0:T(8,128)(2,1)S(1)} %get-tuple-element.121), channel_id=1, source_target_pairs={{1,8},{8,1},{3,10},{10,3},{5,12},{12,5},{7,14},{14,7},{17,24},{24,... | collective-permute-start | bytes 2064392 | tf_op jit(solution)/shard_map/ppermute | solution.py:45
  36.4 3.0 %collective-permute-start.9 = (bf16[21,128,128]{2,1,0:T(8,128)(2,1)S(1)}, bf16[21,128,128]{2,1,0:T(8,128)(2,1)S(1)}, u32[]{:S(2)}, u32[]{:S(2)}) collective-permute-start(bf16[21,128,128]{2,1,0:T(8,128)(2,1)S(1)} %get-tuple-element.122), channel_id=1, source_target_pairs={{1,8},{8,1},{3,10},{10,3},{5,12},{12,5},{7,14},{14,7},{17,24},{24,... | collective-permute-start | bytes 2064392 | tf_op jit(solution)/shard_map/ppermute | solution.py:45
  39.4 1.4 shard_map.77
  40.8 2.1 %shard_map.78 = (bf16[2,1,42,128,128]{4,3,2,1,0:T(8,128)(2,1)}, bf16[84,128,128]{2,1,0:T(8,128)(2,1)S(1)}, bf16[42,128,128]{2,1,0:T(8,128)(2,1)S(1)}, s32[5]{0:T(128)S(1)}) custom-call(s32[5]{0:T(128)S(1)} %get-tuple-element.76.info, s32[9,8]{1,0:T(8,128)S(1)} %copy.14.table, bf16[42,128,128]{2,1,0:T(8,128)(2,1)} %collective-permute-done.1.refs_0_, ...), custom_call_target="tpu_custom_call" | custom-call | tf_op jit(solution)/shard_map/pallas_call | solution.py:374
  42.9 0.8 collective-permute-start.14
  43.8 2.3 %collective-permute-done.10.refs_2_ = bf16[21,128,128]{2,1,0:T(8,128)(2,1)S(1)} collective-permute-done((bf16[21,128,128]{2,1,0:T(8,128)(2,1)S(1)}, bf16[21,128,128]{2,1,0:T(8,128)(2,1)S(1)}, u32[]{:S(2)}, u32[]{:S(2)}) %collective-permute-start.10) | collective-permute-done | bytes 688160 | tf_op jit(solution)/shard_map/ppermute | solution.py:45
  46.1 2.3 %collective-permute-start.12 = (bf16[21,128,128]{2,1,0:T(8,128)(2,1)S(1)}, bf16[21,128,128]{2,1,0:T(8,128)(2,1)S(1)}, u32[]{:S(2)}, u32[]{:S(2)}) collective-permute-start(bf16[21,128,128]{2,1,0:T(8,128)(2,1)S(1)} %collective-permute-done.10.refs_2_), channel_id=1, source_target_pairs={{10,8},{3,1},{12,10},{5,3},{14,12},{7,5},{26,24},{19,17},{28,26},{... | collective-permute-start | bytes 2064392 | tf_op jit(solution)/shard_map/ppermute | solution.py:45
  48.4 5.0 %collective-permute-done.9.refs_1_ = bf16[21,128,128]{2,1,0:T(8,128)(2,1)S(1)} collective-permute-done((bf16[21,128,128]{2,1,0:T(8,128)(2,1)S(1)}, bf16[21,128,128]{2,1,0:T(8,128)(2,1)S(1)}, u32[]{:S(2)}, u32[]{:S(2)}) %collective-permute-start.9) | collective-permute-done | bytes 688160 | tf_op jit(solution)/shard_map/ppermute | solution.py:45
  53.4 2.3 %collective-permute-start.11 = (bf16[21,128,128]{2,1,0:T(8,128)(2,1)S(1)}, bf16[21,128,128]{2,1,0:T(8,128)(2,1)S(1)}, u32[]{:S(2)}, u32[]{:S(2)}) collective-permute-start(bf16[21,128,128]{2,1,0:T(8,128)(2,1)S(1)} %collective-permute-done.9.refs_1_), channel_id=1, source_target_pairs={{10,8},{3,1},{12,10},{5,3},{14,12},{7,5},{26,24},{19,17},{28,26},{... | collective-permute-start | bytes 2064392 | tf_op jit(solution)/shard_map/ppermute | solution.py:45
  55.8 1.3 collective-permute-start.13
  57.1 11.1 %shard_map.79 = (bf16[2,42,128,128]{3,2,1,0:T(8,128)(2,1)S(1)}, s32[5]{0:T(128)S(1)}) custom-call(s32[5]{0:T(128)S(1)} %get-tuple-element.81.info, s32[9,8]{1,0:T(8,128)S(1)} %copy.14.table, bf16[42,128,128]{2,1,0:T(8,128)(2,1)} %collective-permute-done.8.refs_0_, bf16[21,128,128]{2,1,0:T(8,128)(2,1)S(1)} %collective-permute-done.9.refs_1_, ...), custom_call_target="tpu_custom_call" | custom-call | tf_op jit(solution)/shard_map/pallas_call | solution.py:374
  68.2 10.0 %shard_map.80 = (bf16[84,128,128]{2,1,0:T(8,128)(2,1)S(1)}, bf16[42,128,128]{2,1,0:T(8,128)(2,1)S(1)}, bf16[42,128,128]{2,1,0:T(8,128)(2,1)S(1)}, s32[5]{0:T(128)S(1)}) custom-call(s32[5]{0:T(128)S(1)} %get-tuple-element.85.info, s32[9,8]{1,0:T(8,128)S(1)} %copy.14.table, bf16[42,128,128]{2,1,0:T(8,128)(2,1)} %collective-permute-done.2.refs_0_, ...), custom_call_target="tpu_custom_call" | custom-call | tf_op jit(solution)/shard_map/pallas_call | solution.py:374
  78.2 2.3 %collective-permute-start.17 = (bf16[84,128,128]{2,1,0:T(8,128)(2,1)S(1)}, bf16[84,128,128]{2,1,0:T(8,128)(2,1)S(1)}, u32[]{:S(2)}, u32[]{:S(2)}) collective-permute-start(bf16[84,128,128]{2,1,0:T(8,128)(2,1)S(1)} %get-tuple-element.95.refs_0_), channel_id=1, source_target_pairs={{10,8},{3,1},{12,10},{5,3},{14,12},{7,5},{26,24},{19,17},{28,26},{... | collective-permute-start | bytes 8257544 | tf_op jit(solution)/shard_map/ppermute | solution.py:45
  80.5 1.4 collective-permute-start.15
  81.9 2.0 %collective-permute-start.16 = (bf16[42,128,128]{2,1,0:T(8,128)(2,1)S(1)}, bf16[42,128,128]{2,1,0:T(8,128)(2,1)S(1)}, u32[]{:S(2)}, u32[]{:S(2)}) collective-permute-start(bf16[42,128,128]{2,1,0:T(8,128)(2,1)S(1)} %get-tuple-element.102), channel_id=1, source_target_pairs={{8,1},{1,8},{10,3},{3,10},{12,5},{5,12},{14,7},{7,14},{24,17},{17,... | collective-permute-start | bytes 4128776 | tf_op jit(solution)/shard_map/ppermute | solution.py:45
  83.9 1.4 shard_map.81
  85.6 12.1 %shard_map.82 = (bf16[2,42,128,128]{3,2,1,0:T(8,128)(2,1)S(1)}, s32[5]{0:T(128)S(1)}) custom-call(s32[5]{0:T(128)S(1)} %get-tuple-element.94.info, s32[9,8]{1,0:T(8,128)S(1)} %copy.14.table, bf16[84,128,128]{2,1,0:T(8,128)(2,1)S(1)} %get-tuple-element.95.refs_0_, bf16[8,128,128]{2,1,0:T(8,128)(2,1)S(1)} %collective-permute-done.5.refs_3_.refs_1_, ...), custom_call_target="tpu_custom_call" | custom-call | tf_op jit(solution)/shard_map/pallas_call | solution.py:374
  97.7 1.4 shard_map.83
  99.1 1.3 collective-permute-start.18
  100.4 1.2 collective-permute-done.16.refs_2_
  101.6 11.6 %collective-permute-done.17.refs_0_ = bf16[84,128,128]{2,1,0:T(8,128)(2,1)S(1)} collective-permute-done((bf16[84,128,128]{2,1,0:T(8,128)(2,1)S(1)}, bf16[84,128,128]{2,1,0:T(8,128)(2,1)S(1)}, u32[]{:S(2)}, u32[]{:S(2)}) %collective-permute-start.17) | collective-permute-done | bytes 2752544 | tf_op jit(solution)/shard_map/ppermute | solution.py:45
  113.1 9.3 %shard_map.84 = (bf16[42,128,128]{2,1,0:T(8,128)(2,1)S(1)}, bf16[42,128,128]{2,1,0:T(8,128)(2,1)S(1)}, s32[5]{0:T(128)S(1)}) custom-call(s32[5]{0:T(128)S(1)} %get-tuple-element.103.info, s32[9,8]{1,0:T(8,128)S(1)} %copy.14.table, bf16[84,128,128]{2,1,0:T(8,128)(2,1)S(1)} %collective-permute-done.17.refs_0_, ...), custom_call_target="tpu_custom_call" | custom-call | tf_op jit(solution)/shard_map/pallas_call | solution.py:374
  122.4 1.4 collective-permute-start.19
  123.8 1.9 %collective-permute-start.20 = (bf16[42,128,128]{2,1,0:T(8,128)(2,1)S(1)}, bf16[42,128,128]{2,1,0:T(8,128)(2,1)S(1)}, u32[]{:S(2)}, u32[]{:S(2)}) collective-permute-start(bf16[42,128,128]{2,1,0:T(8,128)(2,1)S(1)} %get-tuple-element.110), channel_id=1, source_target_pairs={{8,1},{1,8},{10,3},{3,10},{12,5},{5,12},{14,7},{7,14},{24,17},{17,... | collective-permute-start | bytes 4128776 | tf_op jit(solution)/shard_map/ppermute | solution.py:45
  125.9 1.9 %collective-permute-start.21 = (bf16[42,128,128]{2,1,0:T(8,128)(2,1)S(1)}, bf16[42,128,128]{2,1,0:T(8,128)(2,1)S(1)}, u32[]{:S(2)}, u32[]{:S(2)}) collective-permute-start(bf16[42,128,128]{2,1,0:T(8,128)(2,1)S(1)} %broadcast_select_fusion), channel_id=1, source_target_pairs={{0,8},{2,10},{4,12},{6,14},{9,17},{11,19},{13,21},{15,23},{16,24},... | collective-permute-start | bytes 4128776 | tf_op jit(solution)/shard_map/ppermute | solution.py:45
  127.9 3.8 %shard_map.85 = (bf16[2,1,42,128,128]{4,3,2,1,0:T(8,128)(2,1)}, bf16[2,1,42,128,128]{4,3,2,1,0:T(8,128)(2,1)}) custom-call(s32[5]{0:T(128)S(1)} %get-tuple-element.107.info, bf16[42,128,128]{2,1,0:T(8,128)(2,1)S(1)} %collective-permute-done.13.refs_0_, bf16[42,128,128]{2,1,0:T(8,128)(2,1)S(1)} %collective-permute-done.15.refs_1_, ...), custom_call_target="tpu_custom_call", output_to_operand_aliasing={{0}: (4, {})} | custom-call | tf_op jit(solution)/shard_map/pallas_call | solution.py:431
  131.7 11.7 %collective-permute-done.20.refs_2_ = bf16[42,128,128]{2,1,0:T(8,128)(2,1)S(1)} collective-permute-done((bf16[42,128,128]{2,1,0:T(8,128)(2,1)S(1)}, bf16[42,128,128]{2,1,0:T(8,128)(2,1)S(1)}, u32[]{:S(2)}, u32[]{:S(2)}) %collective-permute-start.20) | collective-permute-done | bytes 1376288 | tf_op jit(solution)/shard_map/ppermute | solution.py:45
  143.4 2.1 %collective-permute-done.21.refs_4_ = bf16[42,128,128]{2,1,0:T(8,128)(2,1)S(1)} collective-permute-done((bf16[42,128,128]{2,1,0:T(8,128)(2,1)S(1)}, bf16[42,128,128]{2,1,0:T(8,128)(2,1)S(1)}, u32[]{:S(2)}, u32[]{:S(2)}) %collective-permute-start.21) | collective-permute-done | bytes 1376288 | tf_op jit(solution)/shard_map/ppermute | solution.py:45
  145.6 2.7 %shard_map.86 = (bf16[2,1,42,128,128]{4,3,2,1,0:T(8,128)(2,1)}, bf16[2,1,42,128,128]{4,3,2,1,0:T(8,128)(2,1)}, bf16[42,128,128]{2,1,0:T(8,128)(2,1)}) custom-call(s32[5]{0:T(128)S(1)} %get-tuple-element.107.info, bf16[42,128,128]{2,1,0:T(8,128)(2,1)S(1)} %collective-permute-done.18.refs_0_, ...), custom_call_target="tpu_custom_call", output_to_operand_aliasing={{0}: (6, {}), {1}: (7, {})} | custom-call | tf_op jit(solution)/shard_map/pallas_call | solution.py:431
  (30 shorter events, 0.6 us)
Async XLA Ops:
  1.6 17.2 %copy-start.2 = (bf16[2,4,128,128]{3,2,1,0:T(8,128)(2,1)}, bf16[2,4,128,128]{3,2,1,0:T(8,128)(2,1)S(1)}, u32[]{:S(2)}) copy-start(bf16[2,4,128,128]{3,2,1,0:T(8,128)(2,1)S(1)} %copy.12) | copy-start | bytes 786436
  1.6 5.5 %copy-start = (bf16[1,1,42,128,128]{4,3,2,1,0:T(8,128)(2,1)S(1)}, bf16[1,1,42,128,128]{4,3,2,1,0:T(8,128)(2,1)}, u32[]{:S(2)}) copy-start(bf16[1,1,42,128,128]{4,3,2,1,0:T(8,128)(2,1)} %param.7) | copy-start | bytes 4128772
  4.4 26.4 %copy-start.6 = (s32[9,8]{0,1:T(8,128)S(1)}, s32[9,8]{0,1:T(8,128)}, u32[]{:S(2)}) copy-start(s32[9,8]{0,1:T(8,128)} %param.9) | copy-start | bytes 868
  4.4 24.4 %collective-permute-start = (bf16[50,128,128]{2,1,0:T(8,128)(2,1)}, bf16[50,128,128]{2,1,0:T(8,128)(2,1)S(1)}, u32[]{:S(2)}, u32[]{:S(2)}) collective-permute-start(bf16[50,128,128]{2,1,0:T(8,128)(2,1)} %pad_maximum_fusion), channel_id=1, source_target_pairs={{1,0},{8,9},{3,2},{10,11},{5,4},{12,13},{7,6},{14,15},{17,16},{24,... | collective-permute-start | bytes 4915208 | tf_op jit(solution)/shard_map/ppermute | solution.py:45
  7.1 18.9 %collective-permute-start.1 = (bf16[42,128,128]{2,1,0:T(8,128)(2,1)S(1)}, bf16[42,128,128]{2,1,0:T(8,128)(2,1)}, u32[]{:S(2)}, u32[]{:S(2)}) collective-permute-start(bf16[42,128,128]{2,1,0:T(8,128)(2,1)S(1)} %bitcast.15), channel_id=1, source_target_pairs={{0,2},{9,11},{2,4},{11,13},{4,6},{13,15},{16,18},{25,27},{18,20},{... | collective-permute-start | bytes 4128776 | tf_op jit(solution)/shard_map/ppermute | solution.py:45
  8.8 19.9 %collective-permute-start.2 = (bf16[42,128,128]{2,1,0:T(8,128)(2,1)}, bf16[42,128,128]{2,1,0:T(8,128)(2,1)}, u32[]{:S(2)}, u32[]{:S(2)}) collective-permute-start(bf16[42,128,128]{2,1,0:T(8,128)(2,1)} %bitcast.9), channel_id=1, source_target_pairs={{2,8},{11,1},{4,10},{13,3},{6,12},{15,5},{18,24},{27,17},{20,26},{... | collective-permute-start | bytes 4128776 | tf_op jit(solution)/shard_map/ppermute | solution.py:45
  14.2 4.7 %collective-permute-start.3 = (bf16[2,168,168]{2,1,0:T(8,128)(2,1)}, bf16[2,168,168]{2,1,0:T(8,128)(2,1)S(1)}, u32[]{:S(2)}, u32[]{:S(2)}) collective-permute-start(bf16[2,168,168]{2,1,0:T(8,128)(2,1)} %reshape.13.own), channel_id=1, source_target_pairs={{0,8},{9,1},{2,10},{11,3},{4,12},{13,5},{6,14},{15,7},{16,24},{25,... | collective-permute-start | bytes 338696 | tf_op jit(solution)/shard_map/ppermute | solution.py:45
  15.5 10.5 %collective-permute-start.5 = (bf16[8,128,128]{2,1,0:T(8,128)(2,1)S(1)}, bf16[8,128,128]{2,1,0:T(8,128)(2,1)S(1)}, u32[]{:S(2)}, u32[]{:S(2)}) collective-permute-start(bf16[8,128,128]{2,1,0:T(8,128)(2,1)S(1)} %bitcast.18), channel_id=1, source_target_pairs={{0,8},{9,1},{2,10},{11,3},{4,12},{13,5},{6,14},{15,7},{16,24},{25,... | collective-permute-start | bytes 786440 | tf_op jit(solution)/shard_map/ppermute | solution.py:45
  18.8 0.7 copy-start.4
  19.5 6.5 %collective-permute-start.4 = (bf16[8,128,128]{2,1,0:T(8,128)(2,1)S(1)}, bf16[8,128,128]{2,1,0:T(8,128)(2,1)}, u32[]{:S(2)}, u32[]{:S(2)}) collective-permute-start(bf16[8,128,128]{2,1,0:T(8,128)(2,1)S(1)} %bitcast.19), channel_id=1, source_target_pairs={{0,2},{9,11},{2,4},{11,13},{4,6},{13,15},{16,18},{25,27},{18,20},{... | collective-permute-start | bytes 786440 | tf_op jit(solution)/shard_map/ppermute | solution.py:45
  21.0 0.9 copy-start.5
  28.8 12.1 %collective-permute-start.7 = (bf16[50,128,128]{2,1,0:T(8,128)(2,1)S(1)}, bf16[50,128,128]{2,1,0:T(8,128)(2,1)S(1)}, u32[]{:S(2)}, u32[]{:S(2)}) collective-permute-start(bf16[50,128,128]{2,1,0:T(8,128)(2,1)S(1)} %collective-permute-done.refs_1_.refs_3_.refs_2_), channel_id=1, source_target_pairs={{0,2},{9,11},{2,4},{11,13},{4,6},{13,15},{16,18},{25,27},{18,20},{... | collective-permute-start | bytes 4915208 | tf_op jit(solution)/shard_map/ppermute | solution.py:45
  29.6 27.5 %collective-permute-start.8 = (bf16[42,128,128]{2,1,0:T(8,128)(2,1)}, bf16[42,128,128]{2,1,0:T(8,128)(2,1)}, u32[]{:S(2)}, u32[]{:S(2)}) collective-permute-start(bf16[42,128,128]{2,1,0:T(8,128)(2,1)} %bitcast.9), channel_id=1, source_target_pairs={{0,8},{9,1},{2,10},{11,3},{4,12},{13,5},{6,14},{15,7},{16,24},{25,... | collective-permute-start | bytes 4128776 | tf_op jit(solution)/shard_map/ppermute | solution.py:45
  31.0 8.4 %copy-start.3 = (bf16[2,4,128,128]{3,2,1,0:T(8,128)(2,1)S(1)}, bf16[2,4,128,128]{3,2,1,0:T(8,128)(2,1)}, u32[]{:S(2)}) copy-start(bf16[2,4,128,128]{3,2,1,0:T(8,128)(2,1)} %copy-done.2) | copy-start | bytes 786436
  31.0 8.4 %collective-permute-start.6 = (bf16[8,128,128]{2,1,0:T(8,128)(2,1)S(1)}, bf16[8,128,128]{2,1,0:T(8,128)(2,1)S(1)}, u32[]{:S(2)}, u32[]{:S(2)}) collective-permute-start(bf16[8,128,128]{2,1,0:T(8,128)(2,1)S(1)} %slice.9), channel_id=1, source_target_pairs={{0,8},{9,1},{2,10},{11,3},{4,12},{13,5},{6,14},{15,7},{16,24},{25,... | collective-permute-start | bytes 786440 | tf_op jit(solution)/shard_map/ppermute | solution.py:45
  33.8 12.3 %collective-permute-start.10 = (bf16[21,128,128]{2,1,0:T(8,128)(2,1)S(1)}, bf16[21,128,128]{2,1,0:T(8,128)(2,1)S(1)}, u32[]{:S(2)}, u32[]{:S(2)}) collective-permute-start(bf16[21,128,128]{2,1,0:T(8,128)(2,1)S(1)} %get-tuple-element.121), channel_id=1, source_target_pairs={{1,8},{8,1},{3,10},{10,3},{5,12},{12,5},{7,14},{14,7},{17,24},{24,... | collective-permute-start | bytes 2064392 | tf_op jit(solution)/shard_map/ppermute | solution.py:45
  36.4 17.1 %collective-permute-start.9 = (bf16[21,128,128]{2,1,0:T(8,128)(2,1)S(1)}, bf16[21,128,128]{2,1,0:T(8,128)(2,1)S(1)}, u32[]{:S(2)}, u32[]{:S(2)}) collective-permute-start(bf16[21,128,128]{2,1,0:T(8,128)(2,1)S(1)} %get-tuple-element.122), channel_id=1, source_target_pairs={{1,8},{8,1},{3,10},{10,3},{5,12},{12,5},{7,14},{14,7},{17,24},{24,... | collective-permute-start | bytes 2064392 | tf_op jit(solution)/shard_map/ppermute | solution.py:45
  42.9 54.7 %collective-permute-start.14 = (bf16[84,128,128]{2,1,0:T(8,128)(2,1)S(1)}, bf16[84,128,128]{2,1,0:T(8,128)(2,1)S(1)}, u32[]{:S(2)}, u32[]{:S(2)}) collective-permute-start(bf16[84,128,128]{2,1,0:T(8,128)(2,1)S(1)} %get-tuple-element.89.refs_0_), channel_id=1, source_target_pairs={{0,2},{9,11},{2,4},{11,13},{4,6},{13,15},{16,18},{25,27},{18,20},{... | collective-permute-start | bytes 8257544 | tf_op jit(solution)/shard_map/ppermute | solution.py:45
  46.1 22.1 %collective-permute-start.12 = (bf16[21,128,128]{2,1,0:T(8,128)(2,1)S(1)}, bf16[21,128,128]{2,1,0:T(8,128)(2,1)S(1)}, u32[]{:S(2)}, u32[]{:S(2)}) collective-permute-start(bf16[21,128,128]{2,1,0:T(8,128)(2,1)S(1)} %collective-permute-done.10.refs_2_), channel_id=1, source_target_pairs={{10,8},{3,1},{12,10},{5,3},{14,12},{7,5},{26,24},{19,17},{28,26},{... | collective-permute-start | bytes 2064392 | tf_op jit(solution)/shard_map/ppermute | solution.py:45
  53.4 14.7 %collective-permute-start.11 = (bf16[21,128,128]{2,1,0:T(8,128)(2,1)S(1)}, bf16[21,128,128]{2,1,0:T(8,128)(2,1)S(1)}, u32[]{:S(2)}, u32[]{:S(2)}) collective-permute-start(bf16[21,128,128]{2,1,0:T(8,128)(2,1)S(1)} %collective-permute-done.9.refs_1_), channel_id=1, source_target_pairs={{10,8},{3,1},{12,10},{5,3},{14,12},{7,5},{26,24},{19,17},{28,26},{... | collective-permute-start | bytes 2064392 | tf_op jit(solution)/shard_map/ppermute | solution.py:45
  55.8 29.8 %collective-permute-start.13 = (bf16[42,128,128]{2,1,0:T(8,128)(2,1)S(1)}, bf16[42,128,128]{2,1,0:T(8,128)(2,1)S(1)}, u32[]{:S(2)}, u32[]{:S(2)}) collective-permute-start(bf16[42,128,128]{2,1,0:T(8,128)(2,1)S(1)} %get-tuple-element.93), channel_id=1, source_target_pairs={{0,1},{9,8},{2,3},{11,10},{4,5},{13,12},{6,7},{15,14},{16,17},{25,... | collective-permute-start | bytes 4128776 | tf_op jit(solution)/shard_map/ppermute | solution.py:45
  78.2 35.0 %collective-permute-start.17 = (bf16[84,128,128]{2,1,0:T(8,128)(2,1)S(1)}, bf16[84,128,128]{2,1,0:T(8,128)(2,1)S(1)}, u32[]{:S(2)}, u32[]{:S(2)}) collective-permute-start(bf16[84,128,128]{2,1,0:T(8,128)(2,1)S(1)} %get-tuple-element.95.refs_0_), channel_id=1, source_target_pairs={{10,8},{3,1},{12,10},{5,3},{14,12},{7,5},{26,24},{19,17},{28,26},{... | collective-permute-start | bytes 8257544 | tf_op jit(solution)/shard_map/ppermute | solution.py:45
  80.5 19.8 %collective-permute-start.15 = (bf16[42,128,128]{2,1,0:T(8,128)(2,1)S(1)}, bf16[42,128,128]{2,1,0:T(8,128)(2,1)S(1)}, u32[]{:S(2)}, u32[]{:S(2)}) collective-permute-start(bf16[42,128,128]{2,1,0:T(8,128)(2,1)S(1)} %get-tuple-element.101), channel_id=1, source_target_pairs={{8,0},{1,9},{10,2},{3,11},{12,4},{5,13},{14,6},{7,15},{24,16},{17,... | collective-permute-start | bytes 4128776 | tf_op jit(solution)/shard_map/ppermute | solution.py:45
  81.9 19.6 %collective-permute-start.16 = (bf16[42,128,128]{2,1,0:T(8,128)(2,1)S(1)}, bf16[42,128,128]{2,1,0:T(8,128)(2,1)S(1)}, u32[]{:S(2)}, u32[]{:S(2)}) collective-permute-start(bf16[42,128,128]{2,1,0:T(8,128)(2,1)S(1)} %get-tuple-element.102), channel_id=1, source_target_pairs={{8,1},{1,8},{10,3},{3,10},{12,5},{5,12},{14,7},{7,14},{24,17},{17,... | collective-permute-start | bytes 4128776 | tf_op jit(solution)/shard_map/ppermute | solution.py:45
  99.1 26.7 %collective-permute-start.18 = (bf16[42,128,128]{2,1,0:T(8,128)(2,1)S(1)}, bf16[42,128,128]{2,1,0:T(8,128)(2,1)S(1)}, u32[]{:S(2)}, u32[]{:S(2)}) collective-permute-start(bf16[42,128,128]{2,1,0:T(8,128)(2,1)S(1)} %get-tuple-element.106), channel_id=1, source_target_pairs={{0,1},{9,8},{2,3},{11,10},{4,5},{13,12},{6,7},{15,14},{16,17},{25,... | collective-permute-start | bytes 4128776 | tf_op jit(solution)/shard_map/ppermute | solution.py:45
  122.4 9.3 %collective-permute-start.19 = (bf16[42,128,128]{2,1,0:T(8,128)(2,1)S(1)}, bf16[42,128,128]{2,1,0:T(8,128)(2,1)S(1)}, u32[]{:S(2)}, u32[]{:S(2)}) collective-permute-start(bf16[42,128,128]{2,1,0:T(8,128)(2,1)S(1)} %get-tuple-element.109), channel_id=1, source_target_pairs={{8,0},{1,9},{10,2},{3,11},{12,4},{5,13},{14,6},{7,15},{24,16},{17,... | collective-permute-start | bytes 4128776 | tf_op jit(solution)/shard_map/ppermute | solution.py:45
  123.8 19.6 %collective-permute-start.20 = (bf16[42,128,128]{2,1,0:T(8,128)(2,1)S(1)}, bf16[42,128,128]{2,1,0:T(8,128)(2,1)S(1)}, u32[]{:S(2)}, u32[]{:S(2)}) collective-permute-start(bf16[42,128,128]{2,1,0:T(8,128)(2,1)S(1)} %get-tuple-element.110), channel_id=1, source_target_pairs={{8,1},{1,8},{10,3},{3,10},{12,5},{5,12},{14,7},{7,14},{24,17},{17,... | collective-permute-start | bytes 4128776 | tf_op jit(solution)/shard_map/ppermute | solution.py:45
  125.9 19.6 %collective-permute-start.21 = (bf16[42,128,128]{2,1,0:T(8,128)(2,1)S(1)}, bf16[42,128,128]{2,1,0:T(8,128)(2,1)S(1)}, u32[]{:S(2)}, u32[]{:S(2)}) collective-permute-start(bf16[42,128,128]{2,1,0:T(8,128)(2,1)S(1)} %broadcast_select_fusion), channel_id=1, source_target_pairs={{0,8},{2,10},{4,12},{6,14},{9,17},{11,19},{13,21},{15,23},{16,24},... | collective-permute-start | bytes 4128776 | tf_op jit(solution)/shard_map/ppermute | solution.py:45
  127.8 17.7 %copy-start.1 = (bf16[1,1,42,128,128]{4,3,2,1,0:T(8,128)(2,1)S(1)}, bf16[1,1,42,128,128]{4,3,2,1,0:T(8,128)(2,1)}, u32[]{:S(2)}) copy-start(bf16[1,1,42,128,128]{4,3,2,1,0:T(8,128)(2,1)} %param.7) | copy-start | bytes 4128772

commit v2 on v1

--- a/solution.py
+++ b/solution.py
@@ -13,6 +13,7 @@
 SUBLANES = 8
 GROUP = SUBLANES // 2
 STEP_ROWS = 2 * SUBLANES
+ROWS_16_BIT = 16
 ANY = pl.BlockSpec(memory_space=pl.ANY)
 SMEM = pl.BlockSpec(memory_space=pltpu.SMEM)
 VMEM = pl.BlockSpec(memory_space=pltpu.VMEM)
@@ -81,7 +82,11 @@
                     )
         i = lax.broadcasted_iota(jnp.int32, out.shape, 0) % GROUP
         j = lax.broadcasted_iota(jnp.int32, out.shape, 1) % GROUP
-        return jnp.where(i == j, out, 0.0).astype(bf16)
+        out = jnp.where(i == j, out, 0.0)
+        more = -out.shape[0] % ROWS_16_BIT
+        if more:
+            out = jnp.concatenate([out, jnp.zeros((more, out.shape[1]), f32)], axis=0)
+        return out.astype(bf16)
 
     def fill(source, flip):
         for step in range(steps):
@@ -101,7 +106,7 @@
 def spread(info, own, received):
     steps, width = own.shape[0], own.shape[1] // 4
     n = width * GROUP
-    shapes = [(n, n), (2 * n, 2 * n), (n, n)] * steps
+    shapes = [(n + -n % ROWS_16_BIT, n), (2 * n + -2 * n % ROWS_16_BIT, 2 * n), (n + -n % ROWS_16_BIT, n)] * steps
     return pl.pallas_call(
         functools.partial(spread_body, width, steps),
         in_specs=[SMEM, VMEM, VMEM],
@@ -261,7 +266,7 @@
                 z[to, :, r, :] = jnp.concatenate([joined_rows(x) for x in halves], axis=1).astype(bf16)
 
             for m, to in ((0, 0), (1, 3)):
-                put(to, [jnp.dot(ks[...], one[2 * h + m], preferred_element_type=f32) for h in range(2)])
+                put(to, [jnp.dot(ks[...], one[2 * h + m], preferred_element_type=f32)[:n] for h in range(2)])
             mixed = [jnp.dot(kd[...], two[h], preferred_element_type=f32) for h in range(2)]
             for t in range(2):
                 put(1 + t, [x[t * n : (t + 1) * n] for x in mixed])
@@ -322,7 +327,7 @@
 
 def terms(left, step, steps, info, table, envs, tensors, small, large, acc=None, onto=None):
     tile = envs[0].shape[-1]
-    width = small.shape[0] // GROUP
+    width = small.shape[1] // GROUP
     last = acc is not None
     final = step + 1 == steps
     pieces = len(envs) - 1
@@ -339,8 +344,8 @@
         pltpu.VMEM((2, width, tile, tile), bf16),
         pltpu.VMEM((4, tile, tile), bf16),
         pltpu.VMEM((4, tile, tile), bf16),
-        pltpu.VMEM((n, n), bf16),
-        pltpu.VMEM((2 * n, 2 * n), bf16),
+        pltpu.VMEM(small.shape, bf16),
+        pltpu.VMEM(large.shape, bf16),
         pltpu.SemaphoreType.DMA((2, 3)),
         pltpu.SemaphoreType.DMA((4,)),
     ]

time: 149 us -> 149 us (level)
  no operation moved by 1% of the time
where the time goes in v2:
time: 149 us; the launch traced here: 148 us
  Pallas kernels  59.3 us (40%)
  waiting for transfers between devices  39 us (26%)
  starting transfers between devices  37.7 us (25%)
  local copies, waits for them, and re-layouts  8.23 us (6%)
  other arithmetic  2.95 us (2%)
    pallas_call x8, Pallas kernels, terms(): pl.pallas_call(body, in_specs=[SMEM, SMEM] + [VMEM if last else ANY] * le...  48.7 us
    ppermute x22, waiting for transfers between devices, move(): return lax.ppermute(block, AXES, route)  39 us
    ppermute x22, starting transfers between devices, move(): return lax.ppermute(block, AXES, route)  37.7 us
    pallas_call x2, Pallas kernels, place(): pl.pallas_call(functools.partial(place_body, plan, len(shapes), [spec is...  6.49 us
    pallas_call x1, Pallas kernels, spread(): pl.pallas_call(functools.partial(spread_body, width, steps), in_specs=[SM...  4.09 us
  transfers between devices with their start and end apart: 22, of which 9 were waited for; matrix products, arithmetic and copies ran while one was open for 4% of the time, Pallas kernels for 38%

profile of v2, /device:TPU:22, one launch (start us, length us, event | category | flops | bytes accessed | tf_op | source)
XLA Modules:
  0.0 148.4 jit_solution(10903548983892688798)
XLA Ops:
  0.6 1.0 copy.12
  1.6 2.8 %pad_maximum_fusion = bf16[50,128,128]{2,1,0:T(8,128)(2,1)} fusion(bf16[8,128,128]{2,1,0:T(8,128)(2,1)S(1)} %bitcast.17, bf16[42,128,128]{2,1,0:T(8,128)(2,1)} %bitcast.13), kind=kLoop, calls=%fused_computation | loop fusion | flops 819200 | bytes 3276800 | tf_op jit(solution)/shard_map/concatenate | solution.py:467
  4.4 2.7 %collective-permute-start = (bf16[50,128,128]{2,1,0:T(8,128)(2,1)}, bf16[50,128,128]{2,1,0:T(8,128)(2,1)S(1)}, u32[]{:S(2)}, u32[]{:S(2)}) collective-permute-start(bf16[50,128,128]{2,1,0:T(8,128)(2,1)} %pad_maximum_fusion), channel_id=1, source_target_pairs={{1,0},{8,9},{3,2},{10,11},{5,4},{12,13},{7,6},{14,15},{17,16},{24,... | collective-permute-start | bytes 4915208 | tf_op jit(solution)/shard_map/ppermute | solution.py:46
  7.1 1.8 %collective-permute-start.1 = (bf16[42,128,128]{2,1,0:T(8,128)(2,1)S(1)}, bf16[42,128,128]{2,1,0:T(8,128)(2,1)}, u32[]{:S(2)}, u32[]{:S(2)}) collective-permute-start(bf16[42,128,128]{2,1,0:T(8,128)(2,1)S(1)} %bitcast.15), channel_id=1, source_target_pairs={{0,2},{9,11},{2,4},{11,13},{4,6},{13,15},{16,18},{25,27},{18,20},{... | collective-permute-start | bytes 4128776 | tf_op jit(solution)/shard_map/ppermute | solution.py:46
  8.8 1.3 collective-permute-start.2
  10.1 2.1 %copy.13 = bf16[2,4,42,4,42]{4,3,2,1,0:T(4,128)(2,1)} copy(bf16[2,4,42,4,42]{2,3,1,4,0:T(4,128)(2,1)} %bitcast.22) | data formatting | bytes 225792 | tf_op jit(solution)/shard_map/transpose | solution.py:452
  12.3 1.9 %reshape.13.own = bf16[2,168,168]{2,1,0:T(8,128)(2,1)} reshape(bf16[2,4,42,4,42]{4,3,2,1,0:T(4,128)(2,1)} %copy.13) | data formatting | bytes 225792 | tf_op jit(solution)/shard_map/reshape | solution.py:452
  14.2 1.3 collective-permute-start.3
  15.5 1.3 collective-permute-start.5
  16.8 2.1 %collective-permute-done.3.received = bf16[2,168,168]{2,1,0:T(8,128)(2,1)S(1)} collective-permute-done((bf16[2,168,168]{2,1,0:T(8,128)(2,1)}, bf16[2,168,168]{2,1,0:T(8,128)(2,1)S(1)}, u32[]{:S(2)}, u32[]{:S(2)}) %collective-permute-start.3) | collective-permute-done | bytes 112928 | tf_op jit(solution)/shard_map/ppermute | solution.py:46
  18.9 0.7 copy-done.4
  19.5 1.4 collective-permute-start.4
  21.0 0.9 copy-done.5
  21.9 4.1 %shard_map.76 = (bf16[176,168]{1,0:T(8,128)(2,1)}, bf16[336,336]{1,0:T(8,128)(2,1)}, bf16[176,168]{1,0:T(8,128)(2,1)}, bf16[176,168]{1,0:T(8,128)(2,1)}, bf16[33...) custom-call(s32[5]{0:T(128)S(1)} %stack.27.info, bf16[2,168,168]{2,1,0:T(8,128)(2,1)} %reshape.13.own, ...), custom_call_target="tpu_custom_call" | custom-call | tf_op jit(solution)/shard_map/pallas_call | solution.py:110
  26.0 2.8 %collective-permute-done.2.refs_0_ = bf16[42,128,128]{2,1,0:T(8,128)(2,1)} collective-permute-done((bf16[42,128,128]{2,1,0:T(8,128)(2,1)}, bf16[42,128,128]{2,1,0:T(8,128)(2,1)}, u32[]{:S(2)}, u32[]{:S(2)}) %collective-permute-start.2) | collective-permute-done | bytes 1376288 | tf_op jit(solution)/shard_map/ppermute | solution.py:46
  28.8 0.8 collective-permute-start.7
  29.6 1.3 collective-permute-start.8
  31.0 1.4 collective-permute-start.6
  32.4 1.4 fusion
  33.8 2.6 %collective-permute-start.10 = (bf16[21,128,128]{2,1,0:T(8,128)(2,1)S(1)}, bf16[21,128,128]{2,1,0:T(8,128)(2,1)S(1)}, u32[]{:S(2)}, u32[]{:S(2)}) collective-permute-start(bf16[21,128,128]{2,1,0:T(8,128)(2,1)S(1)} %get-tuple-element.121), channel_id=1, source_target_pairs={{1,8},{8,1},{3,10},{10,3},{5,12},{12,5},{7,14},{14,7},{17,24},{24,... | collective-permute-start | bytes 2064392 | tf_op jit(solution)/shard_map/ppermute | solution.py:46
  36.4 3.0 %collective-permute-start.9 = (bf16[21,128,128]{2,1,0:T(8,128)(2,1)S(1)}, bf16[21,128,128]{2,1,0:T(8,128)(2,1)S(1)}, u32[]{:S(2)}, u32[]{:S(2)}) collective-permute-start(bf16[21,128,128]{2,1,0:T(8,128)(2,1)S(1)} %get-tuple-element.122), channel_id=1, source_target_pairs={{1,8},{8,1},{3,10},{10,3},{5,12},{12,5},{7,14},{14,7},{17,24},{24,... | collective-permute-start | bytes 2064392 | tf_op jit(solution)/shard_map/ppermute | solution.py:46
  39.4 1.4 shard_map.77
  40.8 2.1 %shard_map.78 = (bf16[2,1,42,128,128]{4,3,2,1,0:T(8,128)(2,1)}, bf16[84,128,128]{2,1,0:T(8,128)(2,1)S(1)}, bf16[42,128,128]{2,1,0:T(8,128)(2,1)S(1)}, s32[5]{0:T(128)S(1)}) custom-call(s32[5]{0:T(128)S(1)} %get-tuple-element.76.info, s32[9,8]{1,0:T(8,128)S(1)} %copy.14.table, bf16[42,128,128]{2,1,0:T(8,128)(2,1)} %collective-permute-done.1.refs_0_, ...), custom_call_target="tpu_custom_call" | custom-call | tf_op jit(solution)/shard_map/pallas_call | solution.py:379
  42.9 0.8 collective-permute-start.14
  43.8 2.3 %collective-permute-done.10.refs_2_ = bf16[21,128,128]{2,1,0:T(8,128)(2,1)S(1)} collective-permute-done((bf16[21,128,128]{2,1,0:T(8,128)(2,1)S(1)}, bf16[21,128,128]{2,1,0:T(8,128)(2,1)S(1)}, u32[]{:S(2)}, u32[]{:S(2)}) %collective-permute-start.10) | collective-permute-done | bytes 688160 | tf_op jit(solution)/shard_map/ppermute | solution.py:46
  46.1 2.3 %collective-permute-start.12 = (bf16[21,128,128]{2,1,0:T(8,128)(2,1)S(1)}, bf16[21,128,128]{2,1,0:T(8,128)(2,1)S(1)}, u32[]{:S(2)}, u32[]{:S(2)}) collective-permute-start(bf16[21,128,128]{2,1,0:T(8,128)(2,1)S(1)} %collective-permute-done.10.refs_2_), channel_id=1, source_target_pairs={{10,8},{3,1},{12,10},{5,3},{14,12},{7,5},{26,24},{19,17},{28,26},{... | collective-permute-start | bytes 2064392 | tf_op jit(solution)/shard_map/ppermute | solution.py:46
  48.4 5.0 %collective-permute-done.9.refs_1_ = bf16[21,128,128]{2,1,0:T(8,128)(2,1)S(1)} collective-permute-done((bf16[21,128,128]{2,1,0:T(8,128)(2,1)S(1)}, bf16[21,128,128]{2,1,0:T(8,128)(2,1)S(1)}, u32[]{:S(2)}, u32[]{:S(2)}) %collective-permute-start.9) | collective-permute-done | bytes 688160 | tf_op jit(solution)/shard_map/ppermute | solution.py:46
  53.4 2.3 %collective-permute-start.11 = (bf16[21,128,128]{2,1,0:T(8,128)(2,1)S(1)}, bf16[21,128,128]{2,1,0:T(8,128)(2,1)S(1)}, u32[]{:S(2)}, u32[]{:S(2)}) collective-permute-start(bf16[21,128,128]{2,1,0:T(8,128)(2,1)S(1)} %collective-permute-done.9.refs_1_), channel_id=1, source_target_pairs={{10,8},{3,1},{12,10},{5,3},{14,12},{7,5},{26,24},{19,17},{28,26},{... | collective-permute-start | bytes 2064392 | tf_op jit(solution)/shard_map/ppermute | solution.py:46
  55.8 1.3 collective-permute-start.13
  57.1 11.1 %shard_map.79 = (bf16[2,42,128,128]{3,2,1,0:T(8,128)(2,1)S(1)}, s32[5]{0:T(128)S(1)}) custom-call(s32[5]{0:T(128)S(1)} %get-tuple-element.81.info, s32[9,8]{1,0:T(8,128)S(1)} %copy.14.table, bf16[42,128,128]{2,1,0:T(8,128)(2,1)} %collective-permute-done.8.refs_0_, bf16[21,128,128]{2,1,0:T(8,128)(2,1)S(1)} %collective-permute-done.9.refs_1_, ...), custom_call_target="tpu_custom_call" | custom-call | tf_op jit(solution)/shard_map/pallas_call | solution.py:379
  68.2 10.0 %shard_map.80 = (bf16[84,128,128]{2,1,0:T(8,128)(2,1)S(1)}, bf16[42,128,128]{2,1,0:T(8,128)(2,1)S(1)}, bf16[42,128,128]{2,1,0:T(8,128)(2,1)S(1)}, s32[5]{0:T(128)S(1)}) custom-call(s32[5]{0:T(128)S(1)} %get-tuple-element.85.info, s32[9,8]{1,0:T(8,128)S(1)} %copy.14.table, bf16[42,128,128]{2,1,0:T(8,128)(2,1)} %collective-permute-done.2.refs_0_, ...), custom_call_target="tpu_custom_call" | custom-call | tf_op jit(solution)/shard_map/pallas_call | solution.py:379
  78.2 2.4 %collective-permute-start.17 = (bf16[84,128,128]{2,1,0:T(8,128)(2,1)S(1)}, bf16[84,128,128]{2,1,0:T(8,128)(2,1)S(1)}, u32[]{:S(2)}, u32[]{:S(2)}) collective-permute-start(bf16[84,128,128]{2,1,0:T(8,128)(2,1)S(1)} %get-tuple-element.95.refs_0_), channel_id=1, source_target_pairs={{10,8},{3,1},{12,10},{5,3},{14,12},{7,5},{26,24},{19,17},{28,26},{... | collective-permute-start | bytes 8257544 | tf_op jit(solution)/shard_map/ppermute | solution.py:46
  80.6 1.4 collective-permute-start.15
  81.9 2.0 %collective-permute-start.16 = (bf16[42,128,128]{2,1,0:T(8,128)(2,1)S(1)}, bf16[42,128,128]{2,1,0:T(8,128)(2,1)S(1)}, u32[]{:S(2)}, u32[]{:S(2)}) collective-permute-start(bf16[42,128,128]{2,1,0:T(8,128)(2,1)S(1)} %get-tuple-element.102), channel_id=1, source_target_pairs={{8,1},{1,8},{10,3},{3,10},{12,5},{5,12},{14,7},{7,14},{24,17},{17,... | collective-permute-start | bytes 4128776 | tf_op jit(solution)/shard_map/ppermute | solution.py:46
  83.9 1.4 shard_map.81
  85.6 12.1 %shard_map.82 = (bf16[2,42,128,128]{3,2,1,0:T(8,128)(2,1)S(1)}, s32[5]{0:T(128)S(1)}) custom-call(s32[5]{0:T(128)S(1)} %get-tuple-element.94.info, s32[9,8]{1,0:T(8,128)S(1)} %copy.14.table, bf16[84,128,128]{2,1,0:T(8,128)(2,1)S(1)} %get-tuple-element.95.refs_0_, bf16[8,128,128]{2,1,0:T(8,128)(2,1)S(1)} %collective-permute-done.5.refs_3_.refs_1_, ...), custom_call_target="tpu_custom_call" | custom-call | tf_op jit(solution)/shard_map/pallas_call | solution.py:379
  97.7 1.4 shard_map.83
  99.1 1.3 collective-permute-start.18
  100.4 1.2 collective-permute-done.16.refs_2_
  101.6 11.6 %collective-permute-done.17.refs_0_ = bf16[84,128,128]{2,1,0:T(8,128)(2,1)S(1)} collective-permute-done((bf16[84,128,128]{2,1,0:T(8,128)(2,1)S(1)}, bf16[84,128,128]{2,1,0:T(8,128)(2,1)S(1)}, u32[]{:S(2)}, u32[]{:S(2)}) %collective-permute-start.17) | collective-permute-done | bytes 2752544 | tf_op jit(solution)/shard_map/ppermute | solution.py:46
  113.1 9.3 %shard_map.84 = (bf16[42,128,128]{2,1,0:T(8,128)(2,1)S(1)}, bf16[42,128,128]{2,1,0:T(8,128)(2,1)S(1)}, s32[5]{0:T(128)S(1)}) custom-call(s32[5]{0:T(128)S(1)} %get-tuple-element.103.info, s32[9,8]{1,0:T(8,128)S(1)} %copy.14.table, bf16[84,128,128]{2,1,0:T(8,128)(2,1)S(1)} %collective-permute-done.17.refs_0_, ...), custom_call_target="tpu_custom_call" | custom-call | tf_op jit(solution)/shard_map/pallas_call | solution.py:379
  122.4 1.4 collective-permute-start.19
  123.8 1.9 %collective-permute-start.20 = (bf16[42,128,128]{2,1,0:T(8,128)(2,1)S(1)}, bf16[42,128,128]{2,1,0:T(8,128)(2,1)S(1)}, u32[]{:S(2)}, u32[]{:S(2)}) collective-permute-start(bf16[42,128,128]{2,1,0:T(8,128)(2,1)S(1)} %get-tuple-element.110), channel_id=1, source_target_pairs={{8,1},{1,8},{10,3},{3,10},{12,5},{5,12},{14,7},{7,14},{24,17},{17,... | collective-permute-start | bytes 4128776 | tf_op jit(solution)/shard_map/ppermute | solution.py:46
  125.9 1.9 %collective-permute-start.21 = (bf16[42,128,128]{2,1,0:T(8,128)(2,1)S(1)}, bf16[42,128,128]{2,1,0:T(8,128)(2,1)S(1)}, u32[]{:S(2)}, u32[]{:S(2)}) collective-permute-start(bf16[42,128,128]{2,1,0:T(8,128)(2,1)S(1)} %broadcast_select_fusion), channel_id=1, source_target_pairs={{0,8},{2,10},{4,12},{6,14},{9,17},{11,19},{13,21},{15,23},{16,24},... | collective-permute-start | bytes 4128776 | tf_op jit(solution)/shard_map/ppermute | solution.py:46
  127.9 3.8 %shard_map.85 = (bf16[2,1,42,128,128]{4,3,2,1,0:T(8,128)(2,1)}, bf16[2,1,42,128,128]{4,3,2,1,0:T(8,128)(2,1)}) custom-call(s32[5]{0:T(128)S(1)} %get-tuple-element.107.info, bf16[42,128,128]{2,1,0:T(8,128)(2,1)S(1)} %collective-permute-done.13.refs_0_, bf16[42,128,128]{2,1,0:T(8,128)(2,1)S(1)} %collective-permute-done.15.refs_1_, ...), custom_call_target="tpu_custom_call", output_to_operand_aliasing={{0}: (4, {})} | custom-call | tf_op jit(solution)/shard_map/pallas_call | solution.py:436
  131.7 11.7 %collective-permute-done.20.refs_2_ = bf16[42,128,128]{2,1,0:T(8,128)(2,1)S(1)} collective-permute-done((bf16[42,128,128]{2,1,0:T(8,128)(2,1)S(1)}, bf16[42,128,128]{2,1,0:T(8,128)(2,1)S(1)}, u32[]{:S(2)}, u32[]{:S(2)}) %collective-permute-start.20) | collective-permute-done | bytes 1376288 | tf_op jit(solution)/shard_map/ppermute | solution.py:46
  143.4 2.1 %collective-permute-done.21.refs_4_ = bf16[42,128,128]{2,1,0:T(8,128)(2,1)S(1)} collective-permute-done((bf16[42,128,128]{2,1,0:T(8,128)(2,1)S(1)}, bf16[42,128,128]{2,1,0:T(8,128)(2,1)S(1)}, u32[]{:S(2)}, u32[]{:S(2)}) %collective-permute-start.21) | collective-permute-done | bytes 1376288 | tf_op jit(solution)/shard_map/ppermute | solution.py:46
  145.5 2.7 %shard_map.86 = (bf16[2,1,42,128,128]{4,3,2,1,0:T(8,128)(2,1)}, bf16[2,1,42,128,128]{4,3,2,1,0:T(8,128)(2,1)}, bf16[42,128,128]{2,1,0:T(8,128)(2,1)}) custom-call(s32[5]{0:T(128)S(1)} %get-tuple-element.107.info, bf16[42,128,128]{2,1,0:T(8,128)(2,1)S(1)} %collective-permute-done.18.refs_0_, ...), custom_call_target="tpu_custom_call", output_to_operand_aliasing={{0}: (6, {}), {1}: (7, {})} | custom-call | tf_op jit(solution)/shard_map/pallas_call | solution.py:436
  (30 shorter events, 0.6 us)
Async XLA Ops:
  1.6 17.2 %copy-start.2 = (bf16[2,4,128,128]{3,2,1,0:T(8,128)(2,1)}, bf16[2,4,128,128]{3,2,1,0:T(8,128)(2,1)S(1)}, u32[]{:S(2)}) copy-start(bf16[2,4,128,128]{3,2,1,0:T(8,128)(2,1)S(1)} %copy.12) | copy-start | bytes 786436
  1.6 5.5 %copy-start = (bf16[1,1,42,128,128]{4,3,2,1,0:T(8,128)(2,1)S(1)}, bf16[1,1,42,128,128]{4,3,2,1,0:T(8,128)(2,1)}, u32[]{:S(2)}) copy-start(bf16[1,1,42,128,128]{4,3,2,1,0:T(8,128)(2,1)} %param.7) | copy-start | bytes 4128772
  4.4 26.4 %copy-start.6 = (s32[9,8]{0,1:T(8,128)S(1)}, s32[9,8]{0,1:T(8,128)}, u32[]{:S(2)}) copy-start(s32[9,8]{0,1:T(8,128)} %param.9) | copy-start | bytes 868
  4.4 24.4 %collective-permute-start = (bf16[50,128,128]{2,1,0:T(8,128)(2,1)}, bf16[50,128,128]{2,1,0:T(8,128)(2,1)S(1)}, u32[]{:S(2)}, u32[]{:S(2)}) collective-permute-start(bf16[50,128,128]{2,1,0:T(8,128)(2,1)} %pad_maximum_fusion), channel_id=1, source_target_pairs={{1,0},{8,9},{3,2},{10,11},{5,4},{12,13},{7,6},{14,15},{17,16},{24,... | collective-permute-start | bytes 4915208 | tf_op jit(solution)/shard_map/ppermute | solution.py:46
  7.1 18.9 %collective-permute-start.1 = (bf16[42,128,128]{2,1,0:T(8,128)(2,1)S(1)}, bf16[42,128,128]{2,1,0:T(8,128)(2,1)}, u32[]{:S(2)}, u32[]{:S(2)}) collective-permute-start(bf16[42,128,128]{2,1,0:T(8,128)(2,1)S(1)} %bitcast.15), channel_id=1, source_target_pairs={{0,2},{9,11},{2,4},{11,13},{4,6},{13,15},{16,18},{25,27},{18,20},{... | collective-permute-start | bytes 4128776 | tf_op jit(solution)/shard_map/ppermute | solution.py:46
  8.8 19.9 %collective-permute-start.2 = (bf16[42,128,128]{2,1,0:T(8,128)(2,1)}, bf16[42,128,128]{2,1,0:T(8,128)(2,1)}, u32[]{:S(2)}, u32[]{:S(2)}) collective-permute-start(bf16[42,128,128]{2,1,0:T(8,128)(2,1)} %bitcast.9), channel_id=1, source_target_pairs={{2,8},{11,1},{4,10},{13,3},{6,12},{15,5},{18,24},{27,17},{20,26},{... | collective-permute-start | bytes 4128776 | tf_op jit(solution)/shard_map/ppermute | solution.py:46
  14.2 4.7 %collective-permute-start.3 = (bf16[2,168,168]{2,1,0:T(8,128)(2,1)}, bf16[2,168,168]{2,1,0:T(8,128)(2,1)S(1)}, u32[]{:S(2)}, u32[]{:S(2)}) collective-permute-start(bf16[2,168,168]{2,1,0:T(8,128)(2,1)} %reshape.13.own), channel_id=1, source_target_pairs={{0,8},{9,1},{2,10},{11,3},{4,12},{13,5},{6,14},{15,7},{16,24},{25,... | collective-permute-start | bytes 338696 | tf_op jit(solution)/shard_map/ppermute | solution.py:46
  15.5 10.5 %collective-permute-start.5 = (bf16[8,128,128]{2,1,0:T(8,128)(2,1)S(1)}, bf16[8,128,128]{2,1,0:T(8,128)(2,1)S(1)}, u32[]{:S(2)}, u32[]{:S(2)}) collective-permute-start(bf16[8,128,128]{2,1,0:T(8,128)(2,1)S(1)} %bitcast.18), channel_id=1, source_target_pairs={{0,8},{9,1},{2,10},{11,3},{4,12},{13,5},{6,14},{15,7},{16,24},{25,... | collective-permute-start | bytes 786440 | tf_op jit(solution)/shard_map/ppermute | solution.py:46
  18.8 0.7 copy-start.4
  19.5 6.5 %collective-permute-start.4 = (bf16[8,128,128]{2,1,0:T(8,128)(2,1)S(1)}, bf16[8,128,128]{2,1,0:T(8,128)(2,1)}, u32[]{:S(2)}, u32[]{:S(2)}) collective-permute-start(bf16[8,128,128]{2,1,0:T(8,128)(2,1)S(1)} %bitcast.19), channel_id=1, source_target_pairs={{0,2},{9,11},{2,4},{11,13},{4,6},{13,15},{16,18},{25,27},{18,20},{... | collective-permute-start | bytes 786440 | tf_op jit(solution)/shard_map/ppermute | solution.py:46
  21.0 0.9 copy-start.5
  28.8 12.1 %collective-permute-start.7 = (bf16[50,128,128]{2,1,0:T(8,128)(2,1)S(1)}, bf16[50,128,128]{2,1,0:T(8,128)(2,1)S(1)}, u32[]{:S(2)}, u32[]{:S(2)}) collective-permute-start(bf16[50,128,128]{2,1,0:T(8,128)(2,1)S(1)} %collective-permute-done.refs_1_.refs_3_.refs_2_), channel_id=1, source_target_pairs={{0,2},{9,11},{2,4},{11,13},{4,6},{13,15},{16,18},{25,27},{18,20},{... | collective-permute-start | bytes 4915208 | tf_op jit(solution)/shard_map/ppermute | solution.py:46
  29.6 27.5 %collective-permute-start.8 = (bf16[42,128,128]{2,1,0:T(8,128)(2,1)}, bf16[42,128,128]{2,1,0:T(8,128)(2,1)}, u32[]{:S(2)}, u32[]{:S(2)}) collective-permute-start(bf16[42,128,128]{2,1,0:T(8,128)(2,1)} %bitcast.9), channel_id=1, source_target_pairs={{0,8},{9,1},{2,10},{11,3},{4,12},{13,5},{6,14},{15,7},{16,24},{25,... | collective-permute-start | bytes 4128776 | tf_op jit(solution)/shard_map/ppermute | solution.py:46
  31.0 8.4 %copy-start.3 = (bf16[2,4,128,128]{3,2,1,0:T(8,128)(2,1)S(1)}, bf16[2,4,128,128]{3,2,1,0:T(8,128)(2,1)}, u32[]{:S(2)}) copy-start(bf16[2,4,128,128]{3,2,1,0:T(8,128)(2,1)} %copy-done.2) | copy-start | bytes 786436
  31.0 8.4 %collective-permute-start.6 = (bf16[8,128,128]{2,1,0:T(8,128)(2,1)S(1)}, bf16[8,128,128]{2,1,0:T(8,128)(2,1)S(1)}, u32[]{:S(2)}, u32[]{:S(2)}) collective-permute-start(bf16[8,128,128]{2,1,0:T(8,128)(2,1)S(1)} %slice.9), channel_id=1, source_target_pairs={{0,8},{9,1},{2,10},{11,3},{4,12},{13,5},{6,14},{15,7},{16,24},{25,... | collective-permute-start | bytes 786440 | tf_op jit(solution)/shard_map/ppermute | solution.py:46
  33.8 12.3 %collective-permute-start.10 = (bf16[21,128,128]{2,1,0:T(8,128)(2,1)S(1)}, bf16[21,128,128]{2,1,0:T(8,128)(2,1)S(1)}, u32[]{:S(2)}, u32[]{:S(2)}) collective-permute-start(bf16[21,128,128]{2,1,0:T(8,128)(2,1)S(1)} %get-tuple-element.121), channel_id=1, source_target_pairs={{1,8},{8,1},{3,10},{10,3},{5,12},{12,5},{7,14},{14,7},{17,24},{24,... | collective-permute-start | bytes 2064392 | tf_op jit(solution)/shard_map/ppermute | solution.py:46
  36.4 17.1 %collective-permute-start.9 = (bf16[21,128,128]{2,1,0:T(8,128)(2,1)S(1)}, bf16[21,128,128]{2,1,0:T(8,128)(2,1)S(1)}, u32[]{:S(2)}, u32[]{:S(2)}) collective-permute-start(bf16[21,128,128]{2,1,0:T(8,128)(2,1)S(1)} %get-tuple-element.122), channel_id=1, source_target_pairs={{1,8},{8,1},{3,10},{10,3},{5,12},{12,5},{7,14},{14,7},{17,24},{24,... | collective-permute-start | bytes 2064392 | tf_op jit(solution)/shard_map/ppermute | solution.py:46
  42.9 54.7 %collective-permute-start.14 = (bf16[84,128,128]{2,1,0:T(8,128)(2,1)S(1)}, bf16[84,128,128]{2,1,0:T(8,128)(2,1)S(1)}, u32[]{:S(2)}, u32[]{:S(2)}) collective-permute-start(bf16[84,128,128]{2,1,0:T(8,128)(2,1)S(1)} %get-tuple-element.89.refs_0_), channel_id=1, source_target_pairs={{0,2},{9,11},{2,4},{11,13},{4,6},{13,15},{16,18},{25,27},{18,20},{... | collective-permute-start | bytes 8257544 | tf_op jit(solution)/shard_map/ppermute | solution.py:46
  46.1 22.1 %collective-permute-start.12 = (bf16[21,128,128]{2,1,0:T(8,128)(2,1)S(1)}, bf16[21,128,128]{2,1,0:T(8,128)(2,1)S(1)}, u32[]{:S(2)}, u32[]{:S(2)}) collective-permute-start(bf16[21,128,128]{2,1,0:T(8,128)(2,1)S(1)} %collective-permute-done.10.refs_2_), channel_id=1, source_target_pairs={{10,8},{3,1},{12,10},{5,3},{14,12},{7,5},{26,24},{19,17},{28,26},{... | collective-permute-start | bytes 2064392 | tf_op jit(solution)/shard_map/ppermute | solution.py:46
  53.4 14.8 %collective-permute-start.11 = (bf16[21,128,128]{2,1,0:T(8,128)(2,1)S(1)}, bf16[21,128,128]{2,1,0:T(8,128)(2,1)S(1)}, u32[]{:S(2)}, u32[]{:S(2)}) collective-permute-start(bf16[21,128,128]{2,1,0:T(8,128)(2,1)S(1)} %collective-permute-done.9.refs_1_), channel_id=1, source_target_pairs={{10,8},{3,1},{12,10},{5,3},{14,12},{7,5},{26,24},{19,17},{28,26},{... | collective-permute-start | bytes 2064392 | tf_op jit(solution)/shard_map/ppermute | solution.py:46
  55.8 29.8 %collective-permute-start.13 = (bf16[42,128,128]{2,1,0:T(8,128)(2,1)S(1)}, bf16[42,128,128]{2,1,0:T(8,128)(2,1)S(1)}, u32[]{:S(2)}, u32[]{:S(2)}) collective-permute-start(bf16[42,128,128]{2,1,0:T(8,128)(2,1)S(1)} %get-tuple-element.93), channel_id=1, source_target_pairs={{0,1},{9,8},{2,3},{11,10},{4,5},{13,12},{6,7},{15,14},{16,17},{25,... | collective-permute-start | bytes 4128776 | tf_op jit(solution)/shard_map/ppermute | solution.py:46
  78.2 35.0 %collective-permute-start.17 = (bf16[84,128,128]{2,1,0:T(8,128)(2,1)S(1)}, bf16[84,128,128]{2,1,0:T(8,128)(2,1)S(1)}, u32[]{:S(2)}, u32[]{:S(2)}) collective-permute-start(bf16[84,128,128]{2,1,0:T(8,128)(2,1)S(1)} %get-tuple-element.95.refs_0_), channel_id=1, source_target_pairs={{10,8},{3,1},{12,10},{5,3},{14,12},{7,5},{26,24},{19,17},{28,26},{... | collective-permute-start | bytes 8257544 | tf_op jit(solution)/shard_map/ppermute | solution.py:46
  80.6 19.8 %collective-permute-start.15 = (bf16[42,128,128]{2,1,0:T(8,128)(2,1)S(1)}, bf16[42,128,128]{2,1,0:T(8,128)(2,1)S(1)}, u32[]{:S(2)}, u32[]{:S(2)}) collective-permute-start(bf16[42,128,128]{2,1,0:T(8,128)(2,1)S(1)} %get-tuple-element.101), channel_id=1, source_target_pairs={{8,0},{1,9},{10,2},{3,11},{12,4},{5,13},{14,6},{7,15},{24,16},{17,... | collective-permute-start | bytes 4128776 | tf_op jit(solution)/shard_map/ppermute | solution.py:46
  81.9 19.6 %collective-permute-start.16 = (bf16[42,128,128]{2,1,0:T(8,128)(2,1)S(1)}, bf16[42,128,128]{2,1,0:T(8,128)(2,1)S(1)}, u32[]{:S(2)}, u32[]{:S(2)}) collective-permute-start(bf16[42,128,128]{2,1,0:T(8,128)(2,1)S(1)} %get-tuple-element.102), channel_id=1, source_target_pairs={{8,1},{1,8},{10,3},{3,10},{12,5},{5,12},{14,7},{7,14},{24,17},{17,... | collective-permute-start | bytes 4128776 | tf_op jit(solution)/shard_map/ppermute | solution.py:46
  99.1 26.7 %collective-permute-start.18 = (bf16[42,128,128]{2,1,0:T(8,128)(2,1)S(1)}, bf16[42,128,128]{2,1,0:T(8,128)(2,1)S(1)}, u32[]{:S(2)}, u32[]{:S(2)}) collective-permute-start(bf16[42,128,128]{2,1,0:T(8,128)(2,1)S(1)} %get-tuple-element.106), channel_id=1, source_target_pairs={{0,1},{9,8},{2,3},{11,10},{4,5},{13,12},{6,7},{15,14},{16,17},{25,... | collective-permute-start | bytes 4128776 | tf_op jit(solution)/shard_map/ppermute | solution.py:46
  122.4 9.3 %collective-permute-start.19 = (bf16[42,128,128]{2,1,0:T(8,128)(2,1)S(1)}, bf16[42,128,128]{2,1,0:T(8,128)(2,1)S(1)}, u32[]{:S(2)}, u32[]{:S(2)}) collective-permute-start(bf16[42,128,128]{2,1,0:T(8,128)(2,1)S(1)} %get-tuple-element.109), channel_id=1, source_target_pairs={{8,0},{1,9},{10,2},{3,11},{12,4},{5,13},{14,6},{7,15},{24,16},{17,... | collective-permute-start | bytes 4128776 | tf_op jit(solution)/shard_map/ppermute | solution.py:46
  123.8 19.6 %collective-permute-start.20 = (bf16[42,128,128]{2,1,0:T(8,128)(2,1)S(1)}, bf16[42,128,128]{2,1,0:T(8,128)(2,1)S(1)}, u32[]{:S(2)}, u32[]{:S(2)}) collective-permute-start(bf16[42,128,128]{2,1,0:T(8,128)(2,1)S(1)} %get-tuple-element.110), channel_id=1, source_target_pairs={{8,1},{1,8},{10,3},{3,10},{12,5},{5,12},{14,7},{7,14},{24,17},{17,... | collective-permute-start | bytes 4128776 | tf_op jit(solution)/shard_map/ppermute | solution.py:46
  125.9 19.6 %collective-permute-start.21 = (bf16[42,128,128]{2,1,0:T(8,128)(2,1)S(1)}, bf16[42,128,128]{2,1,0:T(8,128)(2,1)S(1)}, u32[]{:S(2)}, u32[]{:S(2)}) collective-permute-start(bf16[42,128,128]{2,1,0:T(8,128)(2,1)S(1)} %broadcast_select_fusion), channel_id=1, source_target_pairs={{0,8},{2,10},{4,12},{6,14},{9,17},{11,19},{13,21},{15,23},{16,24},... | collective-permute-start | bytes 4128776 | tf_op jit(solution)/shard_map/ppermute | solution.py:46
  127.8 17.7 %copy-start.1 = (bf16[1,1,42,128,128]{4,3,2,1,0:T(8,128)(2,1)S(1)}, bf16[1,1,42,128,128]{4,3,2,1,0:T(8,128)(2,1)}, u32[]{:S(2)}) copy-start(bf16[1,1,42,128,128]{4,3,2,1,0:T(8,128)(2,1)} %param.7) | copy-start | bytes 4128772

commit v3 on v2

--- a/solution.py
+++ b/solution.py
@@ -534,7 +534,8 @@
     for step, back, backs in kept:
         left_envs, right_envs = place(
             info,
-            [(0, step - 1, [(other, back)]), (1, sites - step, list(zip((own, other), backs)))],
+            [(0, step - 1, [(other, back)]), (1, sites - step, list(zip((own, other), backs)))]
+            + ([(0, step, [(other, left_back)])] if step + 1 == sites else []),
             [envs_shape] * 2,
             [left_envs] + ([] if right_envs is None else [right_envs]),
         )
@@ -546,7 +547,7 @@
     ]
     left_envs, right_envs, left_edge = place(
         info,
-        [(0, sites - 1, [(other, left_back)]), (1, 0, list(zip((own, other), right_back))), (2, None, edge)],
+        ([] if kept else [(0, sites - 1, [(other, left_back)])]) + [(1, 0, list(zip((own, other), right_back))), (2, None, edge)],
         [envs_shape, envs_shape, (width, tile, tile)],
         [left_envs] + ([] if right_envs is None else [right_envs]),
         [left_back, *right_back, edge_tile],

time: 149 us -> 149 us (level)
  transfers between devices with their start and end apart: 22 -> 22, of which waited for: 9 -> 9; matrix products, arithmetic and copies ran while one was open for 4% -> 4% of each run, Pallas kernels for 38% -> 39%
where the time goes in v3:
time: 149 us; the launch traced here: 148 us
  Pallas kernels  60.1 us (40%)
  starting transfers between devices  37.7 us (25%)
  waiting for transfers between devices  37.7 us (25%)
  local copies, waits for them, and re-layouts  8.23 us (6%)
  other arithmetic  2.95 us (2%)
    pallas_call x8, Pallas kernels, terms(): pl.pallas_call(body, in_specs=[SMEM, SMEM] + [VMEM if last else ANY] * le...  48.7 us
    ppermute x22, starting transfers between devices, move(): return lax.ppermute(block, AXES, route)  37.7 us
    ppermute x22, waiting for transfers between devices, move(): return lax.ppermute(block, AXES, route)  37.7 us
    pallas_call x2, Pallas kernels, place(): pl.pallas_call(functools.partial(place_body, plan, len(shapes), [spec is...  7.31 us
    pallas_call x1, Pallas kernels, spread(): pl.pallas_call(functools.partial(spread_body, width, steps), in_specs=[SM...  4.09 us
  transfers between devices with their start and end apart: 22, of which 9 were waited for; matrix products, arithmetic and copies ran while one was open for 4% of the time, Pallas kernels for 39%

profile of v3, /device:TPU:22, one launch (start us, length us, event | category | flops | bytes accessed | tf_op | source)
XLA Modules:
  0.0 147.9 jit_solution(1211560900443129857)
XLA Ops:
  0.6 1.0 copy.12
  1.6 2.8 %pad_maximum_fusion = bf16[50,128,128]{2,1,0:T(8,128)(2,1)} fusion(bf16[8,128,128]{2,1,0:T(8,128)(2,1)S(1)} %bitcast.17, bf16[42,128,128]{2,1,0:T(8,128)(2,1)} %bitcast.13), kind=kLoop, calls=%fused_computation | loop fusion | flops 819200 | bytes 3276800 | tf_op jit(solution)/shard_map/concatenate | solution.py:467
  4.4 2.7 %collective-permute-start = (bf16[50,128,128]{2,1,0:T(8,128)(2,1)}, bf16[50,128,128]{2,1,0:T(8,128)(2,1)S(1)}, u32[]{:S(2)}, u32[]{:S(2)}) collective-permute-start(bf16[50,128,128]{2,1,0:T(8,128)(2,1)} %pad_maximum_fusion), channel_id=1, source_target_pairs={{1,0},{8,9},{3,2},{10,11},{5,4},{12,13},{7,6},{14,15},{17,16},{24,... | collective-permute-start | bytes 4915208 | tf_op jit(solution)/shard_map/ppermute | solution.py:46
  7.1 1.8 %collective-permute-start.1 = (bf16[42,128,128]{2,1,0:T(8,128)(2,1)S(1)}, bf16[42,128,128]{2,1,0:T(8,128)(2,1)}, u32[]{:S(2)}, u32[]{:S(2)}) collective-permute-start(bf16[42,128,128]{2,1,0:T(8,128)(2,1)S(1)} %bitcast.15), channel_id=1, source_target_pairs={{0,2},{9,11},{2,4},{11,13},{4,6},{13,15},{16,18},{25,27},{18,20},{... | collective-permute-start | bytes 4128776 | tf_op jit(solution)/shard_map/ppermute | solution.py:46
  8.8 1.3 collective-permute-start.2
  10.1 2.1 %copy.13 = bf16[2,4,42,4,42]{4,3,2,1,0:T(4,128)(2,1)} copy(bf16[2,4,42,4,42]{2,3,1,4,0:T(4,128)(2,1)} %bitcast.22) | data formatting | bytes 225792 | tf_op jit(solution)/shard_map/transpose | solution.py:452
  12.3 1.9 %reshape.13.own = bf16[2,168,168]{2,1,0:T(8,128)(2,1)} reshape(bf16[2,4,42,4,42]{4,3,2,1,0:T(4,128)(2,1)} %copy.13) | data formatting | bytes 225792 | tf_op jit(solution)/shard_map/reshape | solution.py:452
  14.2 1.3 collective-permute-start.3
  15.5 1.3 collective-permute-start.5
  16.8 2.1 %collective-permute-done.3.received = bf16[2,168,168]{2,1,0:T(8,128)(2,1)S(1)} collective-permute-done((bf16[2,168,168]{2,1,0:T(8,128)(2,1)}, bf16[2,168,168]{2,1,0:T(8,128)(2,1)S(1)}, u32[]{:S(2)}, u32[]{:S(2)}) %collective-permute-start.3) | collective-permute-done | bytes 112928 | tf_op jit(solution)/shard_map/ppermute | solution.py:46
  18.9 0.7 copy-done.4
  19.5 1.4 collective-permute-start.4
  21.0 0.9 copy-done.5
  21.9 4.1 %shard_map.76 = (bf16[176,168]{1,0:T(8,128)(2,1)}, bf16[336,336]{1,0:T(8,128)(2,1)}, bf16[176,168]{1,0:T(8,128)(2,1)}, bf16[176,168]{1,0:T(8,128)(2,1)}, bf16[33...) custom-call(s32[5]{0:T(128)S(1)} %stack.27.info, bf16[2,168,168]{2,1,0:T(8,128)(2,1)} %reshape.13.own, ...), custom_call_target="tpu_custom_call" | custom-call | tf_op jit(solution)/shard_map/pallas_call | solution.py:110
  26.0 2.8 %collective-permute-done.2.refs_0_ = bf16[42,128,128]{2,1,0:T(8,128)(2,1)} collective-permute-done((bf16[42,128,128]{2,1,0:T(8,128)(2,1)}, bf16[42,128,128]{2,1,0:T(8,128)(2,1)}, u32[]{:S(2)}, u32[]{:S(2)}) %collective-permute-start.2) | collective-permute-done | bytes 1376288 | tf_op jit(solution)/shard_map/ppermute | solution.py:46
  28.8 0.8 collective-permute-start.7
  29.6 1.3 collective-permute-start.8
  31.0 1.4 collective-permute-start.6
  32.4 1.4 fusion
  33.8 2.6 %collective-permute-start.10 = (bf16[21,128,128]{2,1,0:T(8,128)(2,1)S(1)}, bf16[21,128,128]{2,1,0:T(8,128)(2,1)S(1)}, u32[]{:S(2)}, u32[]{:S(2)}) collective-permute-start(bf16[21,128,128]{2,1,0:T(8,128)(2,1)S(1)} %get-tuple-element.121), channel_id=1, source_target_pairs={{1,8},{8,1},{3,10},{10,3},{5,12},{12,5},{7,14},{14,7},{17,24},{24,... | collective-permute-start | bytes 2064392 | tf_op jit(solution)/shard_map/ppermute | solution.py:46
  36.4 3.0 %collective-permute-start.9 = (bf16[21,128,128]{2,1,0:T(8,128)(2,1)S(1)}, bf16[21,128,128]{2,1,0:T(8,128)(2,1)S(1)}, u32[]{:S(2)}, u32[]{:S(2)}) collective-permute-start(bf16[21,128,128]{2,1,0:T(8,128)(2,1)S(1)} %get-tuple-element.122), channel_id=1, source_target_pairs={{1,8},{8,1},{3,10},{10,3},{5,12},{12,5},{7,14},{14,7},{17,24},{24,... | collective-permute-start | bytes 2064392 | tf_op jit(solution)/shard_map/ppermute | solution.py:46
  39.4 1.4 shard_map.77
  40.8 2.1 %shard_map.78 = (bf16[2,1,42,128,128]{4,3,2,1,0:T(8,128)(2,1)}, bf16[84,128,128]{2,1,0:T(8,128)(2,1)S(1)}, bf16[42,128,128]{2,1,0:T(8,128)(2,1)S(1)}, s32[5]{0:T(128)S(1)}) custom-call(s32[5]{0:T(128)S(1)} %get-tuple-element.76.info, s32[9,8]{1,0:T(8,128)S(1)} %copy.14.table, bf16[42,128,128]{2,1,0:T(8,128)(2,1)} %collective-permute-done.1.refs_0_, ...), custom_call_target="tpu_custom_call" | custom-call | tf_op jit(solution)/shard_map/pallas_call | solution.py:379
  42.9 0.8 collective-permute-start.14
  43.8 2.3 %collective-permute-done.10.refs_2_ = bf16[21,128,128]{2,1,0:T(8,128)(2,1)S(1)} collective-permute-done((bf16[21,128,128]{2,1,0:T(8,128)(2,1)S(1)}, bf16[21,128,128]{2,1,0:T(8,128)(2,1)S(1)}, u32[]{:S(2)}, u32[]{:S(2)}) %collective-permute-start.10) | collective-permute-done | bytes 688160 | tf_op jit(solution)/shard_map/ppermute | solution.py:46
  46.1 2.3 %collective-permute-start.12 = (bf16[21,128,128]{2,1,0:T(8,128)(2,1)S(1)}, bf16[21,128,128]{2,1,0:T(8,128)(2,1)S(1)}, u32[]{:S(2)}, u32[]{:S(2)}) collective-permute-start(bf16[21,128,128]{2,1,0:T(8,128)(2,1)S(1)} %collective-permute-done.10.refs_2_), channel_id=1, source_target_pairs={{10,8},{3,1},{12,10},{5,3},{14,12},{7,5},{26,24},{19,17},{28,26},{... | collective-permute-start | bytes 2064392 | tf_op jit(solution)/shard_map/ppermute | solution.py:46
  48.4 5.0 %collective-permute-done.9.refs_1_ = bf16[21,128,128]{2,1,0:T(8,128)(2,1)S(1)} collective-permute-done((bf16[21,128,128]{2,1,0:T(8,128)(2,1)S(1)}, bf16[21,128,128]{2,1,0:T(8,128)(2,1)S(1)}, u32[]{:S(2)}, u32[]{:S(2)}) %collective-permute-start.9) | collective-permute-done | bytes 688160 | tf_op jit(solution)/shard_map/ppermute | solution.py:46
  53.4 2.3 %collective-permute-start.11 = (bf16[21,128,128]{2,1,0:T(8,128)(2,1)S(1)}, bf16[21,128,128]{2,1,0:T(8,128)(2,1)S(1)}, u32[]{:S(2)}, u32[]{:S(2)}) collective-permute-start(bf16[21,128,128]{2,1,0:T(8,128)(2,1)S(1)} %collective-permute-done.9.refs_1_), channel_id=1, source_target_pairs={{10,8},{3,1},{12,10},{5,3},{14,12},{7,5},{26,24},{19,17},{28,26},{... | collective-permute-start | bytes 2064392 | tf_op jit(solution)/shard_map/ppermute | solution.py:46
  55.8 1.3 collective-permute-start.13
  57.1 11.1 %shard_map.79 = (bf16[2,42,128,128]{3,2,1,0:T(8,128)(2,1)S(1)}, s32[5]{0:T(128)S(1)}) custom-call(s32[5]{0:T(128)S(1)} %get-tuple-element.81.info, s32[9,8]{1,0:T(8,128)S(1)} %copy.14.table, bf16[42,128,128]{2,1,0:T(8,128)(2,1)} %collective-permute-done.8.refs_0_, bf16[21,128,128]{2,1,0:T(8,128)(2,1)S(1)} %collective-permute-done.9.refs_1_, ...), custom_call_target="tpu_custom_call" | custom-call | tf_op jit(solution)/shard_map/pallas_call | solution.py:379
  68.2 10.0 %shard_map.80 = (bf16[84,128,128]{2,1,0:T(8,128)(2,1)S(1)}, bf16[42,128,128]{2,1,0:T(8,128)(2,1)S(1)}, bf16[42,128,128]{2,1,0:T(8,128)(2,1)S(1)}, s32[5]{0:T(128)S(1)}) custom-call(s32[5]{0:T(128)S(1)} %get-tuple-element.85.info, s32[9,8]{1,0:T(8,128)S(1)} %copy.14.table, bf16[42,128,128]{2,1,0:T(8,128)(2,1)} %collective-permute-done.2.refs_0_, ...), custom_call_target="tpu_custom_call" | custom-call | tf_op jit(solution)/shard_map/pallas_call | solution.py:379
  78.2 2.4 %collective-permute-start.17 = (bf16[84,128,128]{2,1,0:T(8,128)(2,1)S(1)}, bf16[84,128,128]{2,1,0:T(8,128)(2,1)S(1)}, u32[]{:S(2)}, u32[]{:S(2)}) collective-permute-start(bf16[84,128,128]{2,1,0:T(8,128)(2,1)S(1)} %get-tuple-element.95.refs_0_), channel_id=1, source_target_pairs={{10,8},{3,1},{12,10},{5,3},{14,12},{7,5},{26,24},{19,17},{28,26},{... | collective-permute-start | bytes 8257544 | tf_op jit(solution)/shard_map/ppermute | solution.py:46
  80.6 1.4 collective-permute-start.15
  81.9 2.0 %collective-permute-start.16 = (bf16[42,128,128]{2,1,0:T(8,128)(2,1)S(1)}, bf16[42,128,128]{2,1,0:T(8,128)(2,1)S(1)}, u32[]{:S(2)}, u32[]{:S(2)}) collective-permute-start(bf16[42,128,128]{2,1,0:T(8,128)(2,1)S(1)} %get-tuple-element.102), channel_id=1, source_target_pairs={{8,1},{1,8},{10,3},{3,10},{12,5},{5,12},{14,7},{7,14},{24,17},{17,... | collective-permute-start | bytes 4128776 | tf_op jit(solution)/shard_map/ppermute | solution.py:46
  83.9 1.4 shard_map.81
  85.6 12.1 %shard_map.82 = (bf16[2,42,128,128]{3,2,1,0:T(8,128)(2,1)S(1)}, s32[5]{0:T(128)S(1)}) custom-call(s32[5]{0:T(128)S(1)} %get-tuple-element.94.info, s32[9,8]{1,0:T(8,128)S(1)} %copy.14.table, bf16[84,128,128]{2,1,0:T(8,128)(2,1)S(1)} %get-tuple-element.95.refs_0_, bf16[8,128,128]{2,1,0:T(8,128)(2,1)S(1)} %collective-permute-done.5.refs_3_.refs_1_, ...), custom_call_target="tpu_custom_call" | custom-call | tf_op jit(solution)/shard_map/pallas_call | solution.py:379
  97.7 1.4 shard_map.83
  99.1 1.3 collective-permute-start.18
  100.4 1.2 collective-permute-done.16.refs_2_
  101.6 11.6 %collective-permute-done.17.refs_0_ = bf16[84,128,128]{2,1,0:T(8,128)(2,1)S(1)} collective-permute-done((bf16[84,128,128]{2,1,0:T(8,128)(2,1)S(1)}, bf16[84,128,128]{2,1,0:T(8,128)(2,1)S(1)}, u32[]{:S(2)}, u32[]{:S(2)}) %collective-permute-start.17) | collective-permute-done | bytes 2752544 | tf_op jit(solution)/shard_map/ppermute | solution.py:46
  113.1 9.3 %shard_map.84 = (bf16[42,128,128]{2,1,0:T(8,128)(2,1)S(1)}, bf16[42,128,128]{2,1,0:T(8,128)(2,1)S(1)}, s32[5]{0:T(128)S(1)}) custom-call(s32[5]{0:T(128)S(1)} %get-tuple-element.103.info, s32[9,8]{1,0:T(8,128)S(1)} %copy.14.table, bf16[84,128,128]{2,1,0:T(8,128)(2,1)S(1)} %collective-permute-done.17.refs_0_, ...), custom_call_target="tpu_custom_call" | custom-call | tf_op jit(solution)/shard_map/pallas_call | solution.py:379
  122.4 1.4 collective-permute-start.19
  123.8 1.9 %collective-permute-start.20 = (bf16[42,128,128]{2,1,0:T(8,128)(2,1)S(1)}, bf16[42,128,128]{2,1,0:T(8,128)(2,1)S(1)}, u32[]{:S(2)}, u32[]{:S(2)}) collective-permute-start(bf16[42,128,128]{2,1,0:T(8,128)(2,1)S(1)} %get-tuple-element.109), channel_id=1, source_target_pairs={{8,1},{1,8},{10,3},{3,10},{12,5},{5,12},{14,7},{7,14},{24,17},{17,... | collective-permute-start | bytes 4128776 | tf_op jit(solution)/shard_map/ppermute | solution.py:46
  125.9 1.9 %collective-permute-start.21 = (bf16[42,128,128]{2,1,0:T(8,128)(2,1)S(1)}, bf16[42,128,128]{2,1,0:T(8,128)(2,1)S(1)}, u32[]{:S(2)}, u32[]{:S(2)}) collective-permute-start(bf16[42,128,128]{2,1,0:T(8,128)(2,1)S(1)} %broadcast_select_fusion), channel_id=1, source_target_pairs={{0,8},{2,10},{4,12},{6,14},{9,17},{11,19},{13,21},{15,23},{16,24},... | collective-permute-start | bytes 4128776 | tf_op jit(solution)/shard_map/ppermute | solution.py:46
  127.9 5.1 %shard_map.85 = (bf16[2,1,42,128,128]{4,3,2,1,0:T(8,128)(2,1)}, bf16[2,1,42,128,128]{4,3,2,1,0:T(8,128)(2,1)}) custom-call(s32[5]{0:T(128)S(1)} %get-tuple-element.107.info, bf16[42,128,128]{2,1,0:T(8,128)(2,1)S(1)} %collective-permute-done.13.refs_0_, bf16[42,128,128]{2,1,0:T(8,128)(2,1)S(1)} %collective-permute-done.15.refs_1_, ...), custom_call_target="tpu_custom_call", output_to_operand_aliasing={{0}: (5, {})} | custom-call | tf_op jit(solution)/shard_map/pallas_call | solution.py:436
  133.0 10.4 %collective-permute-done.20.refs_1_ = bf16[42,128,128]{2,1,0:T(8,128)(2,1)S(1)} collective-permute-done((bf16[42,128,128]{2,1,0:T(8,128)(2,1)S(1)}, bf16[42,128,128]{2,1,0:T(8,128)(2,1)S(1)}, u32[]{:S(2)}, u32[]{:S(2)}) %collective-permute-start.20) | collective-permute-done | bytes 1376288 | tf_op jit(solution)/shard_map/ppermute | solution.py:46
  143.4 2.1 %collective-permute-done.21.refs_3_ = bf16[42,128,128]{2,1,0:T(8,128)(2,1)S(1)} collective-permute-done((bf16[42,128,128]{2,1,0:T(8,128)(2,1)S(1)}, bf16[42,128,128]{2,1,0:T(8,128)(2,1)S(1)}, u32[]{:S(2)}, u32[]{:S(2)}) %collective-permute-start.21) | collective-permute-done | bytes 1376288 | tf_op jit(solution)/shard_map/ppermute | solution.py:46
  145.5 2.2 %shard_map.86 = (bf16[2,1,42,128,128]{4,3,2,1,0:T(8,128)(2,1)}, bf16[2,1,42,128,128]{4,3,2,1,0:T(8,128)(2,1)}, bf16[42,128,128]{2,1,0:T(8,128)(2,1)}) custom-call(s32[5]{0:T(128)S(1)} %get-tuple-element.107.info, bf16[42,128,128]{2,1,0:T(8,128)(2,1)S(1)} %collective-permute-done.19.refs_0_, ...), custom_call_target="tpu_custom_call", output_to_operand_aliasing={{0}: (5, {}), {1}: (6, {})} | custom-call | tf_op jit(solution)/shard_map/pallas_call | solution.py:436
  (30 shorter events, 0.6 us)
Async XLA Ops:
  1.6 17.2 %copy-start.2 = (bf16[2,4,128,128]{3,2,1,0:T(8,128)(2,1)}, bf16[2,4,128,128]{3,2,1,0:T(8,128)(2,1)S(1)}, u32[]{:S(2)}) copy-start(bf16[2,4,128,128]{3,2,1,0:T(8,128)(2,1)S(1)} %copy.12) | copy-start | bytes 786436
  1.6 5.5 %copy-start = (bf16[1,1,42,128,128]{4,3,2,1,0:T(8,128)(2,1)S(1)}, bf16[1,1,42,128,128]{4,3,2,1,0:T(8,128)(2,1)}, u32[]{:S(2)}) copy-start(bf16[1,1,42,128,128]{4,3,2,1,0:T(8,128)(2,1)} %param.7) | copy-start | bytes 4128772
  4.4 26.4 %copy-start.6 = (s32[9,8]{0,1:T(8,128)S(1)}, s32[9,8]{0,1:T(8,128)}, u32[]{:S(2)}) copy-start(s32[9,8]{0,1:T(8,128)} %param.9) | copy-start | bytes 868
  4.4 24.4 %collective-permute-start = (bf16[50,128,128]{2,1,0:T(8,128)(2,1)}, bf16[50,128,128]{2,1,0:T(8,128)(2,1)S(1)}, u32[]{:S(2)}, u32[]{:S(2)}) collective-permute-start(bf16[50,128,128]{2,1,0:T(8,128)(2,1)} %pad_maximum_fusion), channel_id=1, source_target_pairs={{1,0},{8,9},{3,2},{10,11},{5,4},{12,13},{7,6},{14,15},{17,16},{24,... | collective-permute-start | bytes 4915208 | tf_op jit(solution)/shard_map/ppermute | solution.py:46
  7.1 18.9 %collective-permute-start.1 = (bf16[42,128,128]{2,1,0:T(8,128)(2,1)S(1)}, bf16[42,128,128]{2,1,0:T(8,128)(2,1)}, u32[]{:S(2)}, u32[]{:S(2)}) collective-permute-start(bf16[42,128,128]{2,1,0:T(8,128)(2,1)S(1)} %bitcast.15), channel_id=1, source_target_pairs={{0,2},{9,11},{2,4},{11,13},{4,6},{13,15},{16,18},{25,27},{18,20},{... | collective-permute-start | bytes 4128776 | tf_op jit(solution)/shard_map/ppermute | solution.py:46
  8.8 19.9 %collective-permute-start.2 = (bf16[42,128,128]{2,1,0:T(8,128)(2,1)}, bf16[42,128,128]{2,1,0:T(8,128)(2,1)}, u32[]{:S(2)}, u32[]{:S(2)}) collective-permute-start(bf16[42,128,128]{2,1,0:T(8,128)(2,1)} %bitcast.9), channel_id=1, source_target_pairs={{2,8},{11,1},{4,10},{13,3},{6,12},{15,5},{18,24},{27,17},{20,26},{... | collective-permute-start | bytes 4128776 | tf_op jit(solution)/shard_map/ppermute | solution.py:46
  14.2 4.7 %collective-permute-start.3 = (bf16[2,168,168]{2,1,0:T(8,128)(2,1)}, bf16[2,168,168]{2,1,0:T(8,128)(2,1)S(1)}, u32[]{:S(2)}, u32[]{:S(2)}) collective-permute-start(bf16[2,168,168]{2,1,0:T(8,128)(2,1)} %reshape.13.own), channel_id=1, source_target_pairs={{0,8},{9,1},{2,10},{11,3},{4,12},{13,5},{6,14},{15,7},{16,24},{25,... | collective-permute-start | bytes 338696 | tf_op jit(solution)/shard_map/ppermute | solution.py:46
  15.5 10.5 %collective-permute-start.5 = (bf16[8,128,128]{2,1,0:T(8,128)(2,1)S(1)}, bf16[8,128,128]{2,1,0:T(8,128)(2,1)S(1)}, u32[]{:S(2)}, u32[]{:S(2)}) collective-permute-start(bf16[8,128,128]{2,1,0:T(8,128)(2,1)S(1)} %bitcast.18), channel_id=1, source_target_pairs={{0,8},{9,1},{2,10},{11,3},{4,12},{13,5},{6,14},{15,7},{16,24},{25,... | collective-permute-start | bytes 786440 | tf_op jit(solution)/shard_map/ppermute | solution.py:46
  18.8 0.7 copy-start.4
  19.5 6.5 %collective-permute-start.4 = (bf16[8,128,128]{2,1,0:T(8,128)(2,1)S(1)}, bf16[8,128,128]{2,1,0:T(8,128)(2,1)}, u32[]{:S(2)}, u32[]{:S(2)}) collective-permute-start(bf16[8,128,128]{2,1,0:T(8,128)(2,1)S(1)} %bitcast.19), channel_id=1, source_target_pairs={{0,2},{9,11},{2,4},{11,13},{4,6},{13,15},{16,18},{25,27},{18,20},{... | collective-permute-start | bytes 786440 | tf_op jit(solution)/shard_map/ppermute | solution.py:46
  21.0 0.9 copy-start.5
  28.8 12.1 %collective-permute-start.7 = (bf16[50,128,128]{2,1,0:T(8,128)(2,1)S(1)}, bf16[50,128,128]{2,1,0:T(8,128)(2,1)S(1)}, u32[]{:S(2)}, u32[]{:S(2)}) collective-permute-start(bf16[50,128,128]{2,1,0:T(8,128)(2,1)S(1)} %collective-permute-done.refs_1_.refs_3_.refs_2_), channel_id=1, source_target_pairs={{0,2},{9,11},{2,4},{11,13},{4,6},{13,15},{16,18},{25,27},{18,20},{... | collective-permute-start | bytes 4915208 | tf_op jit(solution)/shard_map/ppermute | solution.py:46
  29.6 27.5 %collective-permute-start.8 = (bf16[42,128,128]{2,1,0:T(8,128)(2,1)}, bf16[42,128,128]{2,1,0:T(8,128)(2,1)}, u32[]{:S(2)}, u32[]{:S(2)}) collective-permute-start(bf16[42,128,128]{2,1,0:T(8,128)(2,1)} %bitcast.9), channel_id=1, source_target_pairs={{0,8},{9,1},{2,10},{11,3},{4,12},{13,5},{6,14},{15,7},{16,24},{25,... | collective-permute-start | bytes 4128776 | tf_op jit(solution)/shard_map/ppermute | solution.py:46
  31.0 8.4 %copy-start.3 = (bf16[2,4,128,128]{3,2,1,0:T(8,128)(2,1)S(1)}, bf16[2,4,128,128]{3,2,1,0:T(8,128)(2,1)}, u32[]{:S(2)}) copy-start(bf16[2,4,128,128]{3,2,1,0:T(8,128)(2,1)} %copy-done.2) | copy-start | bytes 786436
  31.0 8.4 %collective-permute-start.6 = (bf16[8,128,128]{2,1,0:T(8,128)(2,1)S(1)}, bf16[8,128,128]{2,1,0:T(8,128)(2,1)S(1)}, u32[]{:S(2)}, u32[]{:S(2)}) collective-permute-start(bf16[8,128,128]{2,1,0:T(8,128)(2,1)S(1)} %slice.9), channel_id=1, source_target_pairs={{0,8},{9,1},{2,10},{11,3},{4,12},{13,5},{6,14},{15,7},{16,24},{25,... | collective-permute-start | bytes 786440 | tf_op jit(solution)/shard_map/ppermute | solution.py:46
  33.8 12.3 %collective-permute-start.10 = (bf16[21,128,128]{2,1,0:T(8,128)(2,1)S(1)}, bf16[21,128,128]{2,1,0:T(8,128)(2,1)S(1)}, u32[]{:S(2)}, u32[]{:S(2)}) collective-permute-start(bf16[21,128,128]{2,1,0:T(8,128)(2,1)S(1)} %get-tuple-element.121), channel_id=1, source_target_pairs={{1,8},{8,1},{3,10},{10,3},{5,12},{12,5},{7,14},{14,7},{17,24},{24,... | collective-permute-start | bytes 2064392 | tf_op jit(solution)/shard_map/ppermute | solution.py:46
  36.4 17.1 %collective-permute-start.9 = (bf16[21,128,128]{2,1,0:T(8,128)(2,1)S(1)}, bf16[21,128,128]{2,1,0:T(8,128)(2,1)S(1)}, u32[]{:S(2)}, u32[]{:S(2)}) collective-permute-start(bf16[21,128,128]{2,1,0:T(8,128)(2,1)S(1)} %get-tuple-element.122), channel_id=1, source_target_pairs={{1,8},{8,1},{3,10},{10,3},{5,12},{12,5},{7,14},{14,7},{17,24},{24,... | collective-permute-start | bytes 2064392 | tf_op jit(solution)/shard_map/ppermute | solution.py:46
  42.9 54.7 %collective-permute-start.14 = (bf16[84,128,128]{2,1,0:T(8,128)(2,1)S(1)}, bf16[84,128,128]{2,1,0:T(8,128)(2,1)S(1)}, u32[]{:S(2)}, u32[]{:S(2)}) collective-permute-start(bf16[84,128,128]{2,1,0:T(8,128)(2,1)S(1)} %get-tuple-element.89.refs_0_), channel_id=1, source_target_pairs={{0,2},{9,11},{2,4},{11,13},{4,6},{13,15},{16,18},{25,27},{18,20},{... | collective-permute-start | bytes 8257544 | tf_op jit(solution)/shard_map/ppermute | solution.py:46
  46.1 22.1 %collective-permute-start.12 = (bf16[21,128,128]{2,1,0:T(8,128)(2,1)S(1)}, bf16[21,128,128]{2,1,0:T(8,128)(2,1)S(1)}, u32[]{:S(2)}, u32[]{:S(2)}) collective-permute-start(bf16[21,128,128]{2,1,0:T(8,128)(2,1)S(1)} %collective-permute-done.10.refs_2_), channel_id=1, source_target_pairs={{10,8},{3,1},{12,10},{5,3},{14,12},{7,5},{26,24},{19,17},{28,26},{... | collective-permute-start | bytes 2064392 | tf_op jit(solution)/shard_map/ppermute | solution.py:46
  53.4 14.8 %collective-permute-start.11 = (bf16[21,128,128]{2,1,0:T(8,128)(2,1)S(1)}, bf16[21,128,128]{2,1,0:T(8,128)(2,1)S(1)}, u32[]{:S(2)}, u32[]{:S(2)}) collective-permute-start(bf16[21,128,128]{2,1,0:T(8,128)(2,1)S(1)} %collective-permute-done.9.refs_1_), channel_id=1, source_target_pairs={{10,8},{3,1},{12,10},{5,3},{14,12},{7,5},{26,24},{19,17},{28,26},{... | collective-permute-start | bytes 2064392 | tf_op jit(solution)/shard_map/ppermute | solution.py:46
  55.8 29.8 %collective-permute-start.13 = (bf16[42,128,128]{2,1,0:T(8,128)(2,1)S(1)}, bf16[42,128,128]{2,1,0:T(8,128)(2,1)S(1)}, u32[]{:S(2)}, u32[]{:S(2)}) collective-permute-start(bf16[42,128,128]{2,1,0:T(8,128)(2,1)S(1)} %get-tuple-element.93), channel_id=1, source_target_pairs={{0,1},{9,8},{2,3},{11,10},{4,5},{13,12},{6,7},{15,14},{16,17},{25,... | collective-permute-start | bytes 4128776 | tf_op jit(solution)/shard_map/ppermute | solution.py:46
  78.2 35.0 %collective-permute-start.17 = (bf16[84,128,128]{2,1,0:T(8,128)(2,1)S(1)}, bf16[84,128,128]{2,1,0:T(8,128)(2,1)S(1)}, u32[]{:S(2)}, u32[]{:S(2)}) collective-permute-start(bf16[84,128,128]{2,1,0:T(8,128)(2,1)S(1)} %get-tuple-element.95.refs_0_), channel_id=1, source_target_pairs={{10,8},{3,1},{12,10},{5,3},{14,12},{7,5},{26,24},{19,17},{28,26},{... | collective-permute-start | bytes 8257544 | tf_op jit(solution)/shard_map/ppermute | solution.py:46
  80.6 19.8 %collective-permute-start.15 = (bf16[42,128,128]{2,1,0:T(8,128)(2,1)S(1)}, bf16[42,128,128]{2,1,0:T(8,128)(2,1)S(1)}, u32[]{:S(2)}, u32[]{:S(2)}) collective-permute-start(bf16[42,128,128]{2,1,0:T(8,128)(2,1)S(1)} %get-tuple-element.101), channel_id=1, source_target_pairs={{8,0},{1,9},{10,2},{3,11},{12,4},{5,13},{14,6},{7,15},{24,16},{17,... | collective-permute-start | bytes 4128776 | tf_op jit(solution)/shard_map/ppermute | solution.py:46
  81.9 19.6 %collective-permute-start.16 = (bf16[42,128,128]{2,1,0:T(8,128)(2,1)S(1)}, bf16[42,128,128]{2,1,0:T(8,128)(2,1)S(1)}, u32[]{:S(2)}, u32[]{:S(2)}) collective-permute-start(bf16[42,128,128]{2,1,0:T(8,128)(2,1)S(1)} %get-tuple-element.102), channel_id=1, source_target_pairs={{8,1},{1,8},{10,3},{3,10},{12,5},{5,12},{14,7},{7,14},{24,17},{17,... | collective-permute-start | bytes 4128776 | tf_op jit(solution)/shard_map/ppermute | solution.py:46
  99.1 26.7 %collective-permute-start.18 = (bf16[42,128,128]{2,1,0:T(8,128)(2,1)S(1)}, bf16[42,128,128]{2,1,0:T(8,128)(2,1)S(1)}, u32[]{:S(2)}, u32[]{:S(2)}) collective-permute-start(bf16[42,128,128]{2,1,0:T(8,128)(2,1)S(1)} %get-tuple-element.106), channel_id=1, source_target_pairs={{0,1},{9,8},{2,3},{11,10},{4,5},{13,12},{6,7},{15,14},{16,17},{25,... | collective-permute-start | bytes 4128776 | tf_op jit(solution)/shard_map/ppermute | solution.py:46
  122.4 10.6 %collective-permute-start.19 = (bf16[42,128,128]{2,1,0:T(8,128)(2,1)S(1)}, bf16[42,128,128]{2,1,0:T(8,128)(2,1)S(1)}, u32[]{:S(2)}, u32[]{:S(2)}) collective-permute-start(bf16[42,128,128]{2,1,0:T(8,128)(2,1)S(1)} %get-tuple-element.108), channel_id=1, source_target_pairs={{8,0},{1,9},{10,2},{3,11},{12,4},{5,13},{14,6},{7,15},{24,16},{17,... | collective-permute-start | bytes 4128776 | tf_op jit(solution)/shard_map/ppermute | solution.py:46
  123.8 19.6 %collective-permute-start.20 = (bf16[42,128,128]{2,1,0:T(8,128)(2,1)S(1)}, bf16[42,128,128]{2,1,0:T(8,128)(2,1)S(1)}, u32[]{:S(2)}, u32[]{:S(2)}) collective-permute-start(bf16[42,128,128]{2,1,0:T(8,128)(2,1)S(1)} %get-tuple-element.109), channel_id=1, source_target_pairs={{8,1},{1,8},{10,3},{3,10},{12,5},{5,12},{14,7},{7,14},{24,17},{17,... | collective-permute-start | bytes 4128776 | tf_op jit(solution)/shard_map/ppermute | solution.py:46
  125.9 19.6 %collective-permute-start.21 = (bf16[42,128,128]{2,1,0:T(8,128)(2,1)S(1)}, bf16[42,128,128]{2,1,0:T(8,128)(2,1)S(1)}, u32[]{:S(2)}, u32[]{:S(2)}) collective-permute-start(bf16[42,128,128]{2,1,0:T(8,128)(2,1)S(1)} %broadcast_select_fusion), channel_id=1, source_target_pairs={{0,8},{2,10},{4,12},{6,14},{9,17},{11,19},{13,21},{15,23},{16,24},... | collective-permute-start | bytes 4128776 | tf_op jit(solution)/shard_map/ppermute | solution.py:46
  127.8 17.7 %copy-start.1 = (bf16[1,1,42,128,128]{4,3,2,1,0:T(8,128)(2,1)S(1)}, bf16[1,1,42,128,128]{4,3,2,1,0:T(8,128)(2,1)}, u32[]{:S(2)}) copy-start(bf16[1,1,42,128,128]{4,3,2,1,0:T(8,128)(2,1)} %param.7) | copy-start | bytes 4128772
